TPU v7x, 32 devices: a whole 2x2x4 slice. The times are simulated.
32 devices in a mesh: dp: 8 (over z, core), tensor: 4 (over y, x).
Axes of the slice: x: 2, y: 2, z: 4, core: 2. Of those that a mesh axis runs over, the one named last changes fastest.
Arguments:
- tokens: bfloat16 [8192, 2048], P('dp'), may hold values from -6 to 6
- lengths: int32 [8], P('dp'), may hold values from 256 to 1024, as said below
- in_gain: float32 [2048], replicated, may hold values from 0.5 to 1.5
- w_query: bfloat16 [2048, 2048], P(None, 'tensor'), may hold values from -0.125 to 0.125
- w_key: bfloat16 [2048, 1024], P(None, 'tensor'), may hold values from -0.125 to 0.125
- w_value: bfloat16 [2048, 1024], P(None, 'tensor'), may hold values from -0.125 to 0.125
- query_gain: float32 [128], replicated, may hold values from 1 to 2
- key_gain: float32 [128], replicated, may hold values from 1 to 2
- w_out: bfloat16 [2048, 2048], P('tensor'), may hold values from -0.75 to 0.75
- post_gain: float32 [2048], replicated, may hold values from 0.5 to 1.5
- w_gate: bfloat16 [2048, 6144], P(None, 'tensor'), may hold values from -0.125 to 0.125
- w_up: bfloat16 [2048, 6144], P(None, 'tensor'), may hold values from -0.125 to 0.125
- w_down: bfloat16 [6144, 2048], P('tensor'), may hold values from -0.109375 to 0.109375
- out_grad: bfloat16 [8192, 2048], P('dp'), may hold values from -6 to 6
Outputs:
- output: bfloat16 [8192, 2048], P('dp')
- in_grad: bfloat16 [8192, 2048], P('dp')
- grad_in_gain: float32 [2048], replicated
- grad_query: float32 [2048, 2048], P('dp', 'tensor')
- grad_key: float32 [2048, 1024], P('dp', 'tensor')
- grad_value: float32 [2048, 1024], P('dp', 'tensor')
- grad_query_gain: float32 [128], replicated
- grad_key_gain: float32 [128], replicated
- grad_out: float32 [2048, 2048], P('tensor', 'dp')
- grad_post_gain: float32 [2048], replicated
- grad_gate: float32 [2048, 6144], P('dp', 'tensor')
- grad_up: float32 [2048, 6144], P('dp', 'tensor')
- grad_down: float32 [6144, 2048], P('tensor', 'dp')
Inputs may be any that keep to these rules, and one draw needn't show every extreme that they name: `lengths`: valid tokens of each slot of 1024; in every draw some slot is full and some holds exactly 256.
All inputs are finite; a program needn't handle non-finite values.
Results may differ from a plain program's by a relative error of at most 0.024.
Values may be sent and summed in bfloat16 or wider, within the bound.
A program may use at most 256 MiB of HBM per device.

v0:
```python
import jax
import jax.numpy as jnp
from jax import lax
from jax.sharding import PartitionSpec as P

NORM_EPS = 1e-06
ROPE_BASE = 1000000.0
MASK_FILL = -1e30


def unit_rows(matrix):
    return matrix * lax.rsqrt(jnp.mean(matrix * matrix, axis=-1, keepdims=True) + NORM_EPS)


def norm_rows(matrix, scale_gain):
    return unit_rows(matrix) * scale_gain


def rotary(head_width, row_count):
    half_width = head_width // 2
    inv_freq = ROPE_BASE ** (-2.0 * jnp.arange(half_width, dtype=jnp.float32) / head_width)
    angles = jnp.arange(row_count, dtype=jnp.float32)[:, None] * inv_freq[None, :]
    return (jnp.cos(angles), jnp.sin(angles))


def rotate(matrix, cosine, sine_table):
    half_width = matrix.shape[-1] // 2
    first_half = matrix[..., :half_width]
    second_half = matrix[..., half_width:]
    cos_part = cosine[:, None, :]
    sin_part = sine_table[:, None, :]
    return jnp.concatenate(
        [
            first_half * cos_part - second_half * sin_part,
            second_half * cos_part + first_half * sin_part,
        ],
        axis=-1,
    )


def fwd_dot(left, right):
    return jnp.dot(left, right, preferred_element_type=jnp.float32)


def outer_dot(left, right):
    return lax.dot_general(
        left, right, (((0,), (0,)), ((), ())), preferred_element_type=jnp.float32
    )


def back_dot(grad_low, weight):
    return lax.dot_general(
        grad_low, weight, (((1,), (1,)), ((), ())), preferred_element_type=jnp.float32
    )


def masked_scores(query_blk, key_blk, length, offset, score_scale):
    scores = (
        jnp.einsum("qcgd,kcd->cgqk", query_blk, key_blk, preferred_element_type=jnp.float32)
        * score_scale
    )
    q_pos = offset + jnp.arange(query_blk.shape[0], dtype=jnp.int32)
    k_pos = jnp.arange(key_blk.shape[0], dtype=jnp.int32)
    allowed = (k_pos[None, :] <= q_pos[:, None]) & (k_pos[None, :] < length)
    return jnp.where(allowed, scores, MASK_FILL)


def feed_forward(post_unit, post_gain, w_gate, w_up, w_down):
    hidden_in = (post_unit * post_gain).astype(jnp.bfloat16)
    gate_pre = fwd_dot(hidden_in, w_gate)
    up_pre = fwd_dot(hidden_in, w_up)
    gate_sig = jax.nn.sigmoid(gate_pre)
    act_low = (gate_pre * gate_sig * up_pre).astype(jnp.bfloat16)
    return (hidden_in, gate_pre, up_pre, gate_sig, act_low, fwd_dot(act_low, w_down))


def on_device(
    tokens,
    lengths,
    in_gain,
    w_query,
    w_key,
    w_value,
    query_gain,
    key_gain,
    w_out,
    post_gain,
    w_gate,
    w_up,
    w_down,
    out_grad,
):
    seq_count = lengths.shape[0]
    row_count = tokens.shape[0]
    slot_len = row_count // seq_count
    head_width = query_gain.shape[0]
    q_heads = w_query.shape[1] // head_width
    kv_heads = w_key.shape[1] // head_width
    group_size = q_heads // kv_heads
    block_len = min(512, slot_len)
    block_count = slot_len // block_len
    score_scale = head_width ** (-0.5)
    row_index = jnp.arange(row_count, dtype=jnp.int32)
    slot_owner = row_index // slot_len
    position = row_index % slot_len
    owner_hit = slot_owner[:, None] == jnp.arange(seq_count, dtype=jnp.int32)[None, :]
    row_length = jnp.sum(jnp.where(owner_hit, lengths[None, :], 0), axis=1)
    valid_rows = (position < row_length).astype(jnp.float32)[:, None]
    inputs = tokens.astype(jnp.float32)
    in_unit, in_back = jax.vjp(unit_rows, inputs)
    normed = (in_unit * in_gain).astype(jnp.bfloat16)
    q_raw = fwd_dot(normed, w_query)
    k_raw = fwd_dot(normed, w_key)
    values_low = (
        fwd_dot(normed, w_value).astype(jnp.bfloat16).reshape(row_count, kv_heads, head_width)
    )
    cosine, sine_table = rotary(head_width, slot_len)
    cosine = jnp.tile(cosine, (seq_count, 1))
    sine_table = jnp.tile(sine_table, (seq_count, 1))

    def prepare(query_in, key_in, q_gain, k_gain):
        query_heads = norm_rows(query_in.reshape(row_count, q_heads, head_width), q_gain)
        key_heads = norm_rows(key_in.reshape(row_count, kv_heads, head_width), k_gain)
        return (rotate(query_heads, cosine, sine_table), rotate(key_heads, cosine, sine_table))

    (query_rot, key_rot), prep_back = jax.vjp(prepare, q_raw, k_raw, query_gain, key_gain)
    query_low = query_rot.astype(jnp.bfloat16).reshape(row_count, kv_heads, group_size, head_width)
    keys_low = key_rot.astype(jnp.bfloat16)
    pieces = []
    log_totals = []
    seq_index = 0
    key_start = seq_index * slot_len
    for q_block in range(block_count):
        row_start = key_start + q_block * block_len
        key_end = (q_block + 1) * block_len
        scores = masked_scores(
            query_low[row_start : row_start + block_len],
            keys_low[key_start : key_start + key_end],
            lengths[seq_index],
            q_block * block_len,
            score_scale,
        )
        row_peak = jnp.max(scores, axis=-1, keepdims=True)
        exponent = jnp.exp(scores - row_peak)
        row_total = jnp.sum(exponent, axis=-1, keepdims=True)
        probs_low = (exponent / row_total).astype(jnp.bfloat16)
        pieces.append(
            jnp.einsum(
                "cgqk,kcd->qcgd",
                probs_low,
                values_low[key_start : key_start + key_end],
                preferred_element_type=jnp.float32,
            )
        )
        log_totals.append(row_peak + jnp.log(row_total))
    heads_low = (
        jnp.concatenate(pieces, axis=0)
        .reshape(row_count, q_heads * head_width)
        .astype(jnp.bfloat16)
    )
    attn_part = fwd_dot(heads_low, w_out)
    resid = inputs + lax.psum(attn_part.astype(jnp.bfloat16), "tensor").astype(jnp.float32)
    post_unit, post_back = jax.vjp(unit_rows, resid)
    hidden_in, gate_pre, up_pre, gate_sig, act_low, mlp_part = feed_forward(
        post_unit, post_gain, w_gate, w_up, w_down
    )
    mixed = lax.psum(mlp_part.astype(jnp.bfloat16), "tensor").astype(jnp.float32)
    output = (valid_rows * (resid + mixed)).astype(jnp.bfloat16)
    d_out = out_grad.astype(jnp.float32) * valid_rows
    d_out_low = d_out.astype(jnp.bfloat16)
    grad_down = outer_dot(act_low, d_out_low)
    d_act = back_dot(d_out_low, w_down)
    d_gate = (d_act * up_pre * gate_sig * (1.0 + gate_pre * (1.0 - gate_sig))).astype(jnp.bfloat16)
    d_up = (d_act * gate_pre * gate_sig).astype(jnp.bfloat16)
    grad_gate = outer_dot(hidden_in, d_gate)
    grad_up = outer_dot(hidden_in, d_up)
    hidden_part = back_dot(d_gate, w_gate) + back_dot(d_up, w_up)
    post_gain_part = jnp.sum(hidden_part * post_unit, axis=0)
    d_hidden = lax.psum(hidden_part.astype(jnp.bfloat16), "tensor").astype(jnp.float32)
    d_resid = d_out + post_back(d_hidden * post_gain)[0]
    resid_low = d_resid.astype(jnp.bfloat16)
    grad_out = outer_dot(heads_low, resid_low)
    d_heads = (
        back_dot(resid_low, w_out)
        .astype(jnp.bfloat16)
        .reshape(row_count, kv_heads, group_size, head_width)
    )
    q_pieces = []
    seq_index = 0
    key_start = seq_index * slot_len
    key_acc = jnp.zeros((slot_len, kv_heads, head_width), jnp.float32)
    value_acc = jnp.zeros((slot_len, kv_heads, head_width), jnp.float32)
    for q_block in range(block_count):
        row_start = key_start + q_block * block_len
        key_end = (q_block + 1) * block_len
        query_blk = query_low[row_start : row_start + block_len]
        key_blk = keys_low[key_start : key_start + key_end]
        value_blk = values_low[key_start : key_start + key_end]
        grad_blk = d_heads[row_start : row_start + block_len]
        scores = masked_scores(
            query_blk, key_blk, lengths[seq_index], q_block * block_len, score_scale
        )
        probs = jnp.exp(scores - log_totals[seq_index * block_count + q_block])
        probs_low = probs.astype(jnp.bfloat16)
        d_probs = jnp.einsum(
            "qcgd,kcd->cgqk", grad_blk, value_blk, preferred_element_type=jnp.float32
        )
        row_delta = jnp.sum(probs * d_probs, axis=-1, keepdims=True)
        d_scores = (probs * (d_probs - row_delta)).astype(jnp.bfloat16)
        q_pieces.append(
            jnp.einsum("cgqk,kcd->qcgd", d_scores, key_blk, preferred_element_type=jnp.float32)
            * score_scale
        )
        key_acc = key_acc.at[:key_end].add(
            jnp.einsum("cgqk,qcgd->kcd", d_scores, query_blk, preferred_element_type=jnp.float32)
            * score_scale
        )
        value_acc = value_acc.at[:key_end].add(
            jnp.einsum("cgqk,qcgd->kcd", probs_low, grad_blk, preferred_element_type=jnp.float32)
        )
    d_query_rot = jnp.concatenate(q_pieces, axis=0).reshape(row_count, q_heads, head_width)
    d_value = value_acc.reshape(row_count, kv_heads * head_width).astype(jnp.bfloat16)
    d_q_raw, d_k_raw, query_gain_part, key_gain_part = prep_back((d_query_rot, key_acc))
    d_query = d_q_raw.astype(jnp.bfloat16)
    d_key = d_k_raw.astype(jnp.bfloat16)
    grad_query = outer_dot(normed, d_query)
    grad_key = outer_dot(normed, d_key)
    grad_value = outer_dot(normed, d_value)
    normed_part = back_dot(d_query, w_query) + back_dot(d_key, w_key) + back_dot(d_value, w_value)
    in_gain_part = jnp.sum(normed_part * in_unit, axis=0)
    d_normed = lax.psum(normed_part.astype(jnp.bfloat16), "tensor").astype(jnp.float32)
    in_grad = (d_resid + in_back(d_normed * in_gain)[0]).astype(jnp.bfloat16)
    grad_query, grad_key, grad_value, grad_gate, grad_up = (
        lax.psum_scatter(
            grad_query.astype(jnp.bfloat16), "dp", scatter_dimension=0, tiled=True
        ).astype(jnp.float32),
        lax.psum_scatter(
            grad_key.astype(jnp.bfloat16), "dp", scatter_dimension=0, tiled=True
        ).astype(jnp.float32),
        lax.psum_scatter(
            grad_value.astype(jnp.bfloat16), "dp", scatter_dimension=0, tiled=True
        ).astype(jnp.float32),
        lax.psum_scatter(
            grad_gate.astype(jnp.bfloat16), "dp", scatter_dimension=0, tiled=True
        ).astype(jnp.float32),
        lax.psum_scatter(
            grad_up.astype(jnp.bfloat16), "dp", scatter_dimension=0, tiled=True
        ).astype(jnp.float32),
    )
    grad_out, grad_down = (
        lax.psum_scatter(
            grad_out.astype(jnp.bfloat16), "dp", scatter_dimension=1, tiled=True
        ).astype(jnp.float32),
        lax.psum_scatter(
            grad_down.astype(jnp.bfloat16), "dp", scatter_dimension=1, tiled=True
        ).astype(jnp.float32),
    )
    grad_in_gain, grad_query_gain, grad_key_gain, grad_post_gain = lax.psum(
        (in_gain_part, query_gain_part, key_gain_part, post_gain_part), ("dp", "tensor")
    )
    return (
        output,
        in_grad,
        grad_in_gain,
        grad_query,
        grad_key,
        grad_value,
        grad_query_gain,
        grad_key_gain,
        grad_out,
        grad_post_gain,
        grad_gate,
        grad_up,
        grad_down,
    )


def solution(mesh):
    return jax.shard_map(
        on_device,
        mesh=mesh,
        in_specs=(
            P("dp", None),
            P("dp"),
            P(),
            P(None, "tensor"),
            P(None, "tensor"),
            P(None, "tensor"),
            P(),
            P(),
            P("tensor", None),
            P(),
            P(None, "tensor"),
            P(None, "tensor"),
            P("tensor", None),
            P("dp", None),
        ),
        out_specs=(
            P("dp", None),
            P("dp", None),
            P(),
            P("dp", "tensor"),
            P("dp", "tensor"),
            P("dp", "tensor"),
            P(),
            P(),
            P("tensor", "dp"),
            P(),
            P("dp", "tensor"),
            P("dp", "tensor"),
            P("tensor", "dp"),
        ),
        check_vma=False,
    )
```

profile of v0, /device:TPU:0, one launch (start us, length us, event | category | flops | bytes accessed | tf_op | source)
XLA Modules:
  0.0 914.8 jit_solution(13239843963860011807)
XLA Ops:
  8.1 3.1 fusion.7
  12.0 1.9 fusion.66
  15.1 3.3 fusion.2
  18.5 1.3 convolution_convert_fusion.9
  20.6 2.3 multiply_reduce_fusion.8
  22.9 1.6 copy.52
  25.5 2.3 subtract_convert_fusion.1
  27.9 2.4 multiply_reduce_fusion.5
  32.0 1.5 fusion.89
  35.6 1.8 fusion.88
  37.5 1.2 fusion.13
  38.7 2.1 copy-done.3
  40.8 1.6 fusion.60
  43.5 4.4 convolution_convert_fusion.4
  48.2 106.5 %all-reduce.12.cloned.1.call-done = bf16[1024,2048]{1,0:T(8,128)(2,1)} async-done(((bf16[1024,2048]{1,0:T(8,128)(2,1)}), bf16[1024,2048]{1,0:T(8,128)(2,1)}) %all-reduce.12.cloned.1.call-update) | async-done | bytes 4194320 | tf_op jit(solution)/shard_map/psum | solution.py:162
  154.7 5.0 multiply_reduce_fusion.2
  160.6 2.7 multiply_convert_fusion.1
  163.3 12.0 %fusion.93 = f32[1024,1536]{1,0:T(8,128)} fusion(bf16[1024,2048]{1,0:T(8,128)(2,1)S(1)} %multiply_convert_fusion.1, bf16[2048,1536]{1,0:T(8,128)(2,1)} %param.37), kind=kOutput, calls=%fused_computation.174 | convolution fusion | flops 6442450944 | bytes 16777216 | tf_op jit(solution)/shard_map/dot_general | solution.py:42
  175.3 8.7 fusion.92
  184.0 16.1 %multiply_convert_fusion.2 = (bf16[1024,1536]{1,0:T(8,128)(2,1)}, bf16[1024,1536]{1,0:T(8,128)(2,1)}, bf16[1024,1536]{1,0:T(8,128)(2,1)}) fusion(f32[1024,1536]{1,0:T(8,128)} %fusion.92, f32[1024,1536]{1,0:T(8,128)} %fusion.93, bf16[1536,2048]{1,0:T(8,128)(2,1)} %param.38, bf16[1024,2048]{1,0:T(8,128)(2,1)S(1)} %copy-done.32, f32[1024]{0:T(1024)S(1)} %fusion.80), kind=kOutput, calls=%fused_computation.40 | convolution fusion | flops 6473908224 | bytes 32509952 | tf_op jit(solution)/shard_map/dot_general | solution.py:52
  200.1 10.1 %fusion.94 = f32[1024,2048]{1,0:T(8,128)S(1)} fusion(bf16[1024,1536]{1,0:T(8,128)(2,1)} %get-tuple-element.92, bf16[2048,1536]{1,0:T(8,128)(2,1)} %param.36), kind=kOutput, calls=%fused_computation.175 | convolution fusion | flops 6442450944 | bytes 17825792 | tf_op jit(solution)/shard_map/dot_general | solution.py:52
  210.2 12.4 %fusion.90 = (bf16[1024,2048]{1,0:T(8,128)(2,1)}, f32[1024,2048]{1,0:T(8,128)}) fusion(f32[1024,2048]{1,0:T(8,128)S(1)} %fusion.94, bf16[1024,1536]{1,0:T(8,128)(2,1)S(1)} %copy-done.75, bf16[2048,1536]{1,0:T(8,128)(2,1)} %param.37), kind=kOutput, calls=%fused_computation.171 | convolution fusion | flops 6446645248 | bytes 30408704 | tf_op jit(solution)/shard_map/dot_general | solution.py:52
  222.7 103.9 %all-reduce.14.cloned.1.call-done = bf16[1024,2048]{1,0:T(8,128)(2,1)} async-done(((bf16[1024,2048]{1,0:T(8,128)(2,1)}), bf16[1024,2048]{1,0:T(8,128)(2,1)}) %all-reduce.14.cloned.1.call-update) | async-done | bytes 4194320 | tf_op jit(solution)/shard_map/psum | solution.py:179
  326.7 9.0 multiply_reduce_fusion
  336.2 1.2 copy-done.16
  337.3 5.4 fusion.4
  342.8 5.8 fusion.36
  349.5 2.9 fusion.17
  352.5 5.1 fusion.9
  357.5 1.6 fusion.50
  359.9 2.4 convolution_convert_fusion.7
  362.8 4.6 fusion.19
  367.4 7.8 fusion.11
  376.0 1.2 fusion.44
  379.5 1.0 fusion.62
  380.7 4.7 convolution_convert_fusion.8
  385.5 7.5 convolution_convert_fusion.5
  393.3 2.3 fusion.46
  396.1 1.0 fusion.45
  397.7 1.0 copy-done.12
  401.1 1.0 copy-done.31
  402.2 3.8 convolution_convert_fusion.6
  406.0 11.5 %convolution_convert_fusion = bf16[1536,2048]{1,0:T(8,128)(2,1)} fusion(bf16[1024,1536]{1,0:T(8,128)(2,1)} %get-tuple-element.93, bf16[1024,2048]{1,0:T(8,128)(2,1)} %param.39, f32[1024]{0:T(1024)S(1)} %fusion.80), kind=kOutput, calls=%fused_computation.35 | convolution fusion | flops 6451888128 | bytes 13635584 | tf_op jit(solution)/shard_map/dot_general | solution.py:46
  417.9 11.6 %convolution_convert_fusion.1 = bf16[2048,1536]{1,0:T(8,128)(2,1)} fusion(bf16[1024,2048]{1,0:T(8,128)(2,1)} %copy-done.27, bf16[1024,1536]{1,0:T(8,128)(2,1)} %get-tuple-element.91), kind=kOutput, calls=%fused_computation.36 | convolution fusion | flops 6445596672 | bytes 13631488 | tf_op jit(solution)/shard_map/dot_general | solution.py:46
  429.5 11.1 %convolution_convert_fusion.3 = bf16[1024,2048]{1,0:T(8,128)(2,1)} fusion(bf16[1024,1536]{1,0:T(8,128)(2,1)} %get-tuple-element.93, bf16[1536,2048]{1,0:T(8,128)(2,1)} %param.38), kind=kOutput, calls=%fused_computation.57 | convolution fusion | flops 6444548096 | bytes 13631488 | tf_op jit(solution)/shard_map/dot_general | solution.py:42
  440.7 1.3 fusion.96
  442.0 2.4 fusion.95
  444.4 6.2 fusion.91
  450.9 11.7 %convolution_convert_fusion.2 = bf16[2048,1536]{1,0:T(8,128)(2,1)} fusion(bf16[1024,2048]{1,0:T(8,128)(2,1)} %copy-done.27, bf16[1024,1536]{1,0:T(8,128)(2,1)} %get-tuple-element.92), kind=kOutput, calls=%fused_computation.37 | convolution fusion | flops 6445596672 | bytes 13631488 | tf_op jit(solution)/shard_map/dot_general | solution.py:46
  462.7 1.6 convert_element_type.194
  464.4 1.6 convert_element_type.192
  466.0 1.8 convert_element_type.196
  467.8 33.1 %reduce-scatter.8.cloned.1.call-done = bf16[256,512]{1,0:T(8,128)(2,1)} async-done(((bf16[2048,512]{1,0:T(8,128)(2,1)}), bf16[256,512]{1,0:T(8,128)(2,1)}) %reduce-scatter.8.cloned.1.call-update) | async-done | bytes 262160 | tf_op jit(solution)/shard_map/reduce_scatter | solution.py:234
  500.9 1.8 convert_element_type.190
  502.7 69.1 %reduce-scatter.20.cloned.1.call-done = bf16[1536,256]{1,0:T(8,128)(2,1)} async-done(((bf16[1536,2048]{1,0:T(8,128)(2,1)}), bf16[1536,256]{1,0:T(8,128)(2,1)}) %reduce-scatter.20.cloned.1.call-update) | async-done | bytes 786448 | tf_op jit(solution)/shard_map/reduce_scatter | solution.py:254
  571.8 2.4 convert_element_type.202
  574.2 68.1 %reduce-scatter.18.cloned.1.call-done = bf16[256,1536]{1,0:T(8,128)(2,1)} async-done(((bf16[2048,1536]{1,0:T(8,128)(2,1)}), bf16[256,1536]{1,0:T(8,128)(2,1)}) %reduce-scatter.18.cloned.1.call-update) | async-done | bytes 786448 | tf_op jit(solution)/shard_map/reduce_scatter | solution.py:246
  642.3 2.5 convert_element_type.200
  644.7 172.9 %all-reduce.16.cloned.1.call-done = (bf16[1024,2048]{1,0:T(8,128)(2,1)}, bf16[1024,2048]{1,0:T(8,128)(2,1)}) async-done(((bf16[1024,2048]{1,0:T(8,128)(2,1)}, bf16[1024,2048]{1,0:T(8,128)(2,1)}), (bf16[1024,2048]{1,0:T(8,128)(2,1)}, bf16[1024,2048]{1,0:T(8,128)(2,1)})) %all-reduce.16.cloned.1.call-update) | async-done | bytes 8388624 | tf_op jit(solution)/shard_map/psum | solution.py:167
  817.6 7.4 fusion.3
  825.0 42.3 %all-reduce.6 = (f32[2048]{0:T(1024)}, f32[128]{0:T(128)}, f32[128]{0:T(128)}, f32[2048]{0:T(1024)}) all-reduce(f32[2048]{0:T(1024)S(1)} %get-tuple-element.79, f32[128]{0:T(128)S(1)} %get-tuple-element.83, f32[128]{0:T(128)S(1)} %get-tuple-element.81, ...), channel_id=1, replica_groups=mesh['dp'=8,'tensor'=4] {'dp','tensor'}, use_global_device_ids=true, to_apply=%region_19.20 | all-reduce | flops 4352 | bytes 34816 | tf_op jit(solution)/shard_map/psum | solution.py:258
  867.3 24.1 %reduce-scatter.16.cloned.1.call-done = bf16[256,1536]{1,0:T(8,128)(2,1)} async-done(((bf16[2048,1536]{1,0:T(8,128)(2,1)}), bf16[256,1536]{1,0:T(8,128)(2,1)}) %reduce-scatter.16.cloned.1.call-update) | async-done | bytes 786448 | tf_op jit(solution)/shard_map/reduce_scatter | solution.py:243
  891.5 2.5 convert_element_type.198
  893.9 13.5 %fusion.6 = (bf16[1024,2048]{1,0:T(8,128)(2,1)}, bf16[1024,2048]{1,0:T(8,128)(2,1)}) fusion(f32[1024,2048]{1,0:T(8,128)} %copy-done.10, bf16[1024,2048]{1,0:T(8,128)(2,1)} %param.26, bf16[1024,2048]{1,0:T(8,128)(2,1)} %get-tuple-element.90, f32[1024]{0:T(1024)S(1)} %multiply_multiply_fusion.4, f32[2048]{0:T(1024)S(1)} %copy-done.61, f32[1024]{0:T(1024)S(1)} %copy-done.63, ...), kind=kLoop, calls=%fused_computation.13 | loop fusion | flops 31457280 | bytes 33574912 | tf_op jit(solution)/shard_map/convert_element_type | solution.py:232
  (218 shorter events, 20.0 us)
Async XLA Ops:
  7.2 20.6 %copy-start = (bf16[2048,512]{1,0:T(8,128)(2,1)S(1)}, bf16[2048,512]{1,0:T(8,128)(2,1)}, u32[]{:S(2)}) copy-start(bf16[2048,512]{1,0:T(8,128)(2,1)} %param.29) | copy-start | bytes 6291460
  7.2 7.9 copy-start.60
  7.2 147.4 %all-reduce.12.cloned.1.call-start = ((), (), s32[]{:S(2)}) async-start(), calls=%async_computation.7 | async-start | bytes 8388608 | tf_op jit(solution)/shard_map/psum | solution.py:162
  11.2 2.8 copy-start.66
  11.2 7.2 copy-start.62
  14.0 4.4 copy-start.17
  14.0 4.4 copy-start.19
  14.2 17.1 %copy-start.35 = (f32[1024,64]{0,1:T(8,128)}, f32[1024,64]{0,1:T(8,128)S(1)}, u32[]{:S(2)}) copy-start(f32[1024,64]{0,1:T(8,128)S(1)} %copy.53) | copy-start | bytes 786436
  15.1 3.3 copy-start.53
  18.5 2.2 copy-start.28
  19.8 3.1 copy-start.44
  20.6 4.5 copy-start.70
  22.9 4.9 copy-start.68
  24.5 5.8 copy-start.14
  24.5 3.3 copy-start.29
  27.8 7.8 copy-start.21
  27.8 7.8 copy-start.23
  27.9 2.9 copy-start.72
  32.0 2.1 copy-start.25
  32.0 3.6 copy-start.42
  37.5 3.3 copy-start.3
  37.5 3.3 copy-start.45
  40.7 2.8 copy-start.74
  47.9 278.7 %all-reduce.14.cloned.1.call-start = ((), (), s32[]{:S(2)}) async-start(), calls=%async_computation.8 | async-start | bytes 8388608 | tf_op jit(solution)/shard_map/psum | solution.py:179
  48.2 111.5 %copy-start.59 = (f32[2048]{0:T(1024)S(1)}, f32[2048]{0:T(1024)}, u32[]{:S(2)}) copy-start(f32[2048]{0:T(1024)} %param.35) | copy-start | bytes 24580
  154.6 5.1 copy-start.1
  154.7 5.9 copy-start.6
  160.6 14.7 %slice-start.2 = ((s8[6291456]{0:T(1024)(128)(4,1)}), s8[2097152]{0:T(1024)(128)(4,1)S(1)}, s32[]{:S(2)}) async-start(s8[6291456]{0:T(1024)(128)(4,1)} %bitcast.205), calls=%async_computation.19 | async-start | bytes 4194304
  163.3 12.1 %copy-start.27 = (bf16[1024,2048]{1,0:T(8,128)(2,1)}, bf16[1024,2048]{1,0:T(8,128)(2,1)S(1)}, u32[]{:S(2)}) copy-start(bf16[1024,2048]{1,0:T(8,128)(2,1)S(1)} %multiply_convert_fusion.1) | copy-start | bytes 12582916
  163.3 12.0 %slice-start.3 = ((s8[6291456]{0:T(1024)(128)(4,1)}), s8[4194304]{0:T(1024)(128)(4,1)S(1)}, s32[]{:S(2)}) async-start(s8[6291456]{0:T(1024)(128)(4,1)} %bitcast.205), calls=%async_computation.20 | async-start | bytes 8388608
  175.3 8.7 copy-start.32
  200.1 10.1 %copy-start.75 = (bf16[1024,1536]{1,0:T(8,128)(2,1)S(1)}, bf16[1024,1536]{1,0:T(8,128)(2,1)}, u32[]{:S(2)}) copy-start(bf16[1024,1536]{1,0:T(8,128)(2,1)} %get-tuple-element.91) | copy-start | bytes 9437188
  222.7 240.1 %reduce-scatter.12.cloned.1.call-start = ((), (), s32[]{:S(2)}) async-start(), calls=%async_computation.11 | async-start | bytes 1179648 | tf_op jit(solution)/shard_map/reduce_scatter | solution.py:240
  326.7 9.0 copy-start.2
  326.7 9.5 %copy-start.7 = (bf16[1024,2048]{1,0:T(8,128)(2,1)S(1)}, bf16[1024,2048]{1,0:T(8,128)(2,1)}, u32[]{:S(2)}) copy-start(bf16[1024,2048]{1,0:T(8,128)(2,1)} %all-reduce.12.cloned.1.call-done) | copy-start | bytes 12582916
  326.7 10.7 %copy-start.16 = (bf16[1024,2048]{1,0:T(8,128)(2,1)S(1)}, bf16[1024,2048]{1,0:T(8,128)(2,1)}, u32[]{:S(2)}) copy-start(bf16[1024,2048]{1,0:T(8,128)(2,1)} %all-reduce.14.cloned.1.call-done) | copy-start | bytes 12582916
  337.3 15.1 %slice-start = ((s8[8388608]{0:T(1024)(128)(4,1)}), s8[4194304]{0:T(1024)(128)(4,1)S(1)}, s32[]{:S(2)}) async-start(s8[8388608]{0:T(1024)(128)(4,1)} %bitcast.180), calls=%async_computation.17 | async-start | bytes 8388608
  342.7 5.8 copy-start.10
  342.7 5.9 copy-start.5
  342.8 9.7 %slice-start.1 = ((s8[8388608]{0:T(1024)(128)(4,1)}), s8[4194304]{0:T(1024)(128)(4,1)S(1)}, s32[]{:S(2)}) async-start(s8[8388608]{0:T(1024)(128)(4,1)} %bitcast.180), calls=%async_computation.18 | async-start | bytes 8388608
  349.5 2.9 copy-start.46
  357.5 2.4 copy-start.30
  362.3 102.0 %reduce-scatter.10.cloned.1.call-start = ((), (), s32[]{:S(2)}) async-start(), calls=%async_computation.10 | async-start | bytes 1179648 | tf_op jit(solution)/shard_map/reduce_scatter | solution.py:237
  367.4 7.8 copy-start.13
  367.4 7.8 copy-start.26
  367.4 8.6 copy-start.43
  380.7 4.7 copy-start.33
  385.5 7.8 copy-start.22
  385.5 7.8 copy-start.24
  385.5 80.5 %reduce-scatter.14.cloned.1.call-start = ((), (), s32[]{:S(2)}) async-start(), calls=%async_computation.12 | async-start | bytes 2359296 | tf_op jit(solution)/shard_map/reduce_scatter | solution.py:251
  393.0 107.9 %reduce-scatter.8.cloned.1.call-start = ((), (), s32[]{:S(2)}) async-start(), calls=%async_computation.9 | async-start | bytes 2359296 | tf_op jit(solution)/shard_map/reduce_scatter | solution.py:234
  393.2 2.9 copy-start.9
  399.5 2.6 copy-start.31
  406.0 165.8 %reduce-scatter.20.cloned.1.call-start = ((), (), s32[]{:S(2)}) async-start(), calls=%async_computation.15 | async-start | bytes 7077888 | tf_op jit(solution)/shard_map/reduce_scatter | solution.py:254
  417.6 224.7 %reduce-scatter.18.cloned.1.call-start = ((), (), s32[]{:S(2)}) async-start(), calls=%async_computation.14 | async-start | bytes 7077888 | tf_op jit(solution)/shard_map/reduce_scatter | solution.py:246
  429.5 11.2 %copy-start.34 = (bf16[1024,2,128]{0,2,1:T(8,128)(2,1)S(1)}, bf16[1024,2,128]{0,2,1:T(8,128)(2,1)}, u32[]{:S(2)}) copy-start(bf16[1024,2,128]{0,2,1:T(8,128)(2,1)} %copy-done.33) | copy-start | bytes 1572868
  429.5 388.1 %all-reduce.16.cloned.1.call-start = ((), (), s32[]{:S(2)}) async-start(), calls=%async_computation.16 | async-start | bytes 16777216 | tf_op jit(solution)/shard_map/psum | solution.py:167
  429.5 11.1 %copy-start.48 = (bf16[2048,256]{1,0:T(8,128)(2,1)S(1)}, bf16[2048,256]{1,0:T(8,128)(2,1)}, u32[]{:S(2)}) copy-start(bf16[2048,256]{1,0:T(8,128)(2,1)} %param.30) | copy-start | bytes 3145732
  442.0 2.4 copy-start.41
  442.0 2.4 copy-start.54
  450.6 440.8 %reduce-scatter.16.cloned.1.call-start = ((), (), s32[]{:S(2)}) async-start(), calls=%async_computation.13 | async-start | bytes 7077888 | tf_op jit(solution)/shard_map/reduce_scatter | solution.py:243
  462.7 354.9 %copy-start.61 = (f32[2048]{0:T(1024)S(1)}, f32[2048]{0:T(1024)}, u32[]{:S(2)}) copy-start(f32[2048]{0:T(1024)} %param.28) | copy-start | bytes 24580
  462.7 354.9 %copy-start.63 = (f32[1024]{0:T(1024)S(1)}, f32[1024]{0:T(1024)}, u32[]{:S(2)}) copy-start(f32[1024]{0:T(1024)} %copy-done.62) | copy-start | bytes 12292
  817.6 49.7 %copy-start.67 = (f32[1024]{0:T(1024)S(1)}, f32[1024]{0:T(1024)}, u32[]{:S(2)}) copy-start(f32[1024]{0:T(1024)} %copy-done.66) | copy-start | bytes 12292
  (26 other events, 38.9 us)
Sparse Core Ops, SparseCore 0:
  48.1 106.5 all-reduce.11
  222.8 103.8 all-reduce.13
  362.4 32.1 reduce-scatter.11
  397.4 30.6 reduce-scatter.9
  430.2 34.1 reduce-scatter.13
  466.6 34.2 reduce-scatter.7
  503.2 68.5 reduce-scatter.19
  574.1 68.1 reduce-scatter.17
  646.6 170.9 all-reduce.15
  819.9 71.5 reduce-scatter.15
where the time goes:
time: 924 us; the launch traced here: 915 us
  waiting for transfers between devices  578 us (63%)
  matrix products  171 us (19%)
  other arithmetic  89 us (10%)
  blocking collectives  42.3 us (5%)
  between operations  16.6 us (2%)
  local copies, waits for them, and re-layouts  16 us (2%)
    psum x1, waiting for transfers between devices, on_device(): lax.psum(mlp_part.astype(jnp.bfloat16), 'tensor').astype(jnp.float32)  173 us
    psum x1, waiting for transfers between devices, on_device(): lax.psum(attn_part.astype(jnp.bfloat16), 'tensor').astype(jnp.float32)  106 us
    psum x1, waiting for transfers between devices, on_device(): lax.psum(hidden_part.astype(jnp.bfloat16), 'tensor').astype(jnp.float32)  104 us
    reduce_scatter x1, waiting for transfers between devices, on_device(): lax.psum_scatter(grad_down.astype(jnp.bfloat16), 'dp', scatter_dimension=...  69.1 us
    reduce_scatter x1, waiting for transfers between devices, on_device(): lax.psum_scatter(grad_up.astype(jnp.bfloat16), 'dp', scatter_dimension=0,...  68.1 us
    dot_general x7, matrix products, back_dot(): lax.dot_general(grad_low, weight, (((1,), (1,)), ((), ())), preferred_ele...  54.2 us
    dot_general x7, matrix products, outer_dot(): lax.dot_general(left, right, (((0,), (0,)), ((), ())), preferred_element_...  53.2 us
    psum x1, blocking collectives, on_device(): lax.psum((in_gain_part, query_gain_part, key_gain_part, post_gain_part),...  42.3 us
  transfers between devices with their start and end apart: 10, of which 7 were waited for; matrix products, arithmetic and copies ran while one was open for 12% of the time, Pallas kernels for 0%

commit v1 on v0

v1 whole, which is shorter than its diff:
```python
import functools

import jax
import jax.numpy as jnp
from jax import lax
from jax.experimental import pallas as pl
from jax.experimental.pallas import tpu as pltpu
from jax.sharding import PartitionSpec as P

NORM_EPS = 1e-06
ROPE_BASE = 1000000.0
MASK_FILL = -1e30
LOW = jnp.bfloat16
F32 = jnp.float32
MESH = pl.DeviceIdType.MESH
VMEM_BYTES = 60 * 1024 * 1024
SUBS = 2


def unit_rows(matrix):
    return matrix * lax.rsqrt(jnp.mean(matrix * matrix, axis=-1, keepdims=True) + NORM_EPS)


def norm_rows(matrix, scale_gain):
    return unit_rows(matrix) * scale_gain


def rotary(head_width, row_count):
    half_width = head_width // 2
    inv_freq = ROPE_BASE ** (-2.0 * jnp.arange(half_width, dtype=F32) / head_width)
    angles = jnp.arange(row_count, dtype=F32)[:, None] * inv_freq[None, :]
    return (jnp.cos(angles), jnp.sin(angles))


def rotate(matrix, cosine, sine_table):
    half_width = matrix.shape[-1] // 2
    first_half = matrix[..., :half_width]
    second_half = matrix[..., half_width:]
    cos_part = cosine[:, None, :]
    sin_part = sine_table[:, None, :]
    return jnp.concatenate(
        [
            first_half * cos_part - second_half * sin_part,
            second_half * cos_part + first_half * sin_part,
        ],
        axis=-1,
    )


def dot_nn(left, right):
    return jnp.dot(left, right, preferred_element_type=F32)


def dot_tn(left, right):
    return lax.dot_general(left, right, (((0,), (0,)), ((), ())), preferred_element_type=F32)


def dot_nt(left, right):
    return lax.dot_general(left, right, (((1,), (1,)), ((), ())), preferred_element_type=F32)


def masked_scores(query_blk, key_blk, length, offset, score_scale):
    scores = (
        jnp.einsum("qcgd,kcd->cgqk", query_blk, key_blk, preferred_element_type=F32) * score_scale
    )
    q_pos = offset + jnp.arange(query_blk.shape[0], dtype=jnp.int32)
    k_pos = jnp.arange(key_blk.shape[0], dtype=jnp.int32)
    allowed = (k_pos[None, :] <= q_pos[:, None]) & (k_pos[None, :] < length)
    return jnp.where(allowed, scores, MASK_FILL)


class Swap:
    def __init__(self, count, rows, width):
        self.count, self.width = count, width
        self.bits = count.bit_length() - 1
        self.block = rows // count
        self.sub = self.block // SUBS
        self.half = width // 2
        self.orders = [list(range(self.bits)), list(range(self.bits))[::-1]]
        self.slots = []
        for order in self.orders:
            slot = {}
            for step in range(self.bits):
                for r in range(count):
                    if not any(r >> b & 1 for b in order[: step + 1]):
                        slot[step, r] = len(slot)
            self.slots.append(slot)

    def scratch(self):
        n = self.count
        return [
            pltpu.VMEM((2, n - 1, self.block, self.half), LOW),
            pltpu.SemaphoreType.DMA((2, n, SUBS)),
            pltpu.SemaphoreType.DMA((2, n, SUBS)),
            pltpu.SemaphoreType.DMA((2, n * self.bits, SUBS)),
            pltpu.SemaphoreType.DMA((2, n, SUBS)),
        ]

    def bind(self, part, recv, scatter_send, scatter_recv, gather_send, gather_recv, dest):
        self.part, self.recv, self.dest = part, recv, dest
        self.sems = scatter_send, scatter_recv, gather_send, gather_recv
        self.me = lax.axis_index("tensor")

    def near(self, bit):
        own = (self.me // 2**bit) % 2
        return self.me + (1 - 2 * own) * 2**bit

    def rows(self, r, sub=None):
        owner = self.me
        for bit in range(self.bits):
            if r >> bit & 1:
                own = (self.me // 2**bit) % 2
                owner = owner + (1 - 2 * own) * 2**bit
        start = owner * self.block
        if sub is None:
            return pl.ds(pl.multiple_of(start, self.block), self.block)
        return pl.ds(pl.multiple_of(start + sub * self.sub, self.sub), self.sub)

    def columns(self, half):
        return pl.ds(half * self.half, self.half)

    def greet(self):
        barrier = pltpu.get_barrier_semaphore()
        for bit in range(self.bits):
            pl.semaphore_signal(
                barrier, inc=1, device_id={"tensor": self.near(bit)}, device_id_type=MESH
            )
        pl.semaphore_wait(barrier, self.bits)

    def first(self, half, r):
        return next(k for k, bit in enumerate(self.orders[half]) if r >> bit & 1)

    def scatter_copy(self, half, r, sub):
        step = self.first(half, r)
        bit = self.orders[half][step]
        slot = self.slots[half][step, r ^ (1 << bit)]
        return pltpu.make_async_remote_copy(
            src_ref=self.part.at[self.rows(r, sub), self.columns(half)],
            dst_ref=self.recv.at[half, slot, pl.ds(sub * self.sub, self.sub)],
            send_sem=self.sems[0].at[half, r, sub],
            recv_sem=self.sems[1].at[half, slot, sub],
            device_id={"tensor": self.near(bit)},
            device_id_type=MESH,
        )

    def scatter_wait(self, half, step, r, sub):
        slot = self.slots[half][step, r]
        ref = self.recv.at[half, slot, pl.ds(sub * self.sub, self.sub)]
        pltpu.make_async_copy(ref, ref, self.sems[1].at[half, slot, sub]).wait()
        return ref

    def scatter_start(self, r):
        for sub in range(SUBS):
            for half in range(2):
                if self.first(half, r) == 0:
                    self.scatter_copy(half, r, sub).start()

    def scatter_forward(self, half, r):
        step = self.first(half, r)
        for sub in range(SUBS):
            where = self.rows(r, sub), self.columns(half)
            total = self.part[where].astype(F32)
            for j in range(step):
                total = total + self.scatter_wait(half, j, r, sub)[...].astype(F32)
            self.part[where] = total.astype(LOW)
            self.scatter_copy(half, r, sub).start()

    def forwards(self):
        todo = [
            (self.first(half, r), half, r)
            for half in range(2)
            for r in range(1, self.count)
            if self.first(half, r) > 0
        ]
        return [(half, r) for _, half, r in sorted(todo)]

    def scatter_result(self, sub):
        total = []
        for half in range(2):
            value = self.part[self.rows(0, sub), self.columns(half)].astype(F32)
            for j in range(self.bits):
                value = value + self.scatter_wait(half, j, 0, sub)[...].astype(F32)
            total.append(value)
        return jnp.concatenate(total, axis=1)

    def scatter_end(self):
        for half in range(2):
            for r in range(1, self.count):
                for sub in range(SUBS):
                    self.scatter_copy(half, r, sub).wait_send()

    def last(self, half, r):
        order = self.orders[half][::-1]
        return max([-1] + [j for j, bit in enumerate(order) if r >> bit & 1])

    def gather_copy(self, half, r, step, sub, source=None):
        bit = self.orders[half][::-1][step]
        where = self.rows(r, sub), self.columns(half)
        return pltpu.make_async_remote_copy(
            src_ref=self.dest.at[where],
            dst_ref=self.dest.at[where],
            send_sem=self.sems[2].at[half, r * self.bits + step, sub],
            recv_sem=self.sems[3].at[half, r ^ (1 << bit), sub],
            device_id={"tensor": self.near(bit)},
            device_id_type=MESH,
        )

    def gather_start(self, sub):
        for step in range(self.bits):
            for half in range(2):
                self.gather_copy(half, 0, step, sub).start()

    def gather_wait(self, half, r, sub):
        ref = self.dest.at[self.rows(r, sub), self.columns(half)]
        pltpu.make_async_copy(ref, ref, self.sems[3].at[half, r, sub]).wait()

    def gather_steps(self):
        todo = [
            (self.last(half, r), sub, bin(r).count("1"), half, r)
            for half in range(2)
            for r in range(1, self.count)
            for sub in range(SUBS)
        ]
        return [(half, r, sub) for _, sub, _, half, r in sorted(todo)]

    def gather_pass(self, half, r, sub):
        self.gather_wait(half, r, sub)
        for step in range(self.last(half, r) + 1, self.bits):
            self.gather_copy(half, r, step, sub).start()

    def gather_end(self):
        for half in range(2):
            for r in range(self.count):
                for step in range(self.last(half, r) + 1, self.bits):
                    for sub in range(SUBS):
                        self.gather_copy(half, r, step, sub).wait_send()

    def order(self):
        return sorted(range(self.count), key=lambda r: (-bin(r).count("1"), r))


def tiled(total, size, body):
    count = total // size

    def step(i, carry):
        body(pl.ds(pl.multiple_of(i * size, size), size))
        return carry

    lax.fori_loop(0, count, step, 0)


def any_spec():
    return pl.BlockSpec(memory_space=pl.ANY)


def vmem_spec():
    return pl.BlockSpec(memory_space=pltpu.VMEM)


def kernel_params(identity):
    return pltpu.CompilerParams(
        collective_id=identity, has_side_effects=True, vmem_limit_bytes=VMEM_BYTES
    )


def out_kernel(
    swap, heads_ref, w_ref, x_ref, gain_ref, resid_ref, hidden_ref, part, dest, local_sem, *comm
):
    swap.bind(part, *comm, dest)
    swap.greet()
    for r in swap.order():
        rows = swap.rows(r)

        def columns(cols):
            part[rows, cols] = dot_nn(heads_ref[rows, :], w_ref[:, cols]).astype(LOW)

        tiled(swap.width, 512, columns)
        if r:
            swap.scatter_start(r)
    for half, r in swap.forwards():
        swap.scatter_forward(half, r)
    for sub in range(SUBS):
        local = pl.ds(sub * swap.sub, swap.sub)
        resid = x_ref[local, :].astype(F32) + swap.scatter_result(sub)
        resid_ref[local, :] = resid
        dest[swap.rows(0, sub), :] = (unit_rows(resid) * gain_ref[...]).astype(LOW)
        swap.gather_start(sub)
    for half, r, sub in swap.gather_steps():
        swap.gather_pass(half, r, sub)
    swap.scatter_end()
    swap.gather_end()
    copy = pltpu.make_async_copy(dest, hidden_ref, local_sem)
    copy.start()
    copy.wait()


def out_sum(count, heads, w_out, x_rows, gain):
    rows, width = heads.shape[0], w_out.shape[1]
    swap = Swap(count, rows, width)
    return pl.pallas_call(
        functools.partial(out_kernel, swap),
        out_shape=(
            jax.ShapeDtypeStruct((swap.block, width), F32),
            jax.ShapeDtypeStruct((rows, width), LOW),
        ),
        in_specs=[vmem_spec()] * 4,
        out_specs=(vmem_spec(), any_spec()),
        scratch_shapes=[
            pltpu.VMEM((rows, width), LOW),
            pltpu.VMEM((rows, width), LOW),
            pltpu.SemaphoreType.DMA,
            *swap.scratch(),
        ],
        compiler_params=kernel_params(0),
        name="out_sum",
    )(heads, w_out, x_rows, gain[None, :])


def feed_kernel(
    swap,
    shards,
    hidden_hbm,
    grad_hbm,
    wg_hbm,
    wu_hbm,
    wd_hbm,
    resid_ref,
    gain_ref,
    act_out,
    gg_out,
    gu_out,
    gd_out,
    d_resid_ref,
    low_out,
    gain_part_ref,
    hidden,
    grad,
    wg,
    wu,
    wd,
    act,
    dg,
    du,
    part,
    dest,
    stage,
    in_sems,
    stage_sems,
    out_sems,
    *comm,
):
    swap.bind(part, *comm, dest)
    loads = [
        pltpu.make_async_copy(src, dst, in_sems.at[i])
        for i, (src, dst) in enumerate(
            [(hidden_hbm, hidden), (wg_hbm, wg), (wu_hbm, wu), (grad_hbm, grad), (wd_hbm, wd)]
        )
    ]
    for load in loads:
        load.start()
    swap.greet()
    for load in loads:
        load.wait()
    units = wg.shape[1]
    unit_tile = 512 if units % 512 == 0 else 256
    forwards = swap.forwards()
    order = swap.order()
    for place, r in enumerate(order):
        rows = swap.rows(r)

        def unit_step(cols):
            gate = dot_nn(hidden[rows, :], wg[:, cols])
            up = dot_nn(hidden[rows, :], wu[:, cols])
            d_act = dot_nt(grad[rows, :], wd[cols, :])
            sig = jax.nn.sigmoid(gate)
            silu = gate * sig
            act[rows, cols] = (silu * up).astype(LOW)
            dg[rows, cols] = (d_act * up * sig * (1.0 + gate * (1.0 - sig))).astype(LOW)
            du[rows, cols] = (d_act * silu).astype(LOW)

        tiled(units, unit_tile, unit_step)

        def back_step(cols):
            part[rows, cols] = (
                dot_nt(dg[rows, :], wg[cols, :]) + dot_nt(du[rows, :], wu[cols, :])
            ).astype(LOW)

        tiled(swap.width, 512, back_step)
        if r:
            swap.scatter_start(r)
        if place == len(order) - 2:
            for half, s in forwards:
                swap.scatter_forward(half, s)
    act_copy = pltpu.make_async_copy(act, act_out, in_sems.at[0])
    act_copy.start()

    def weight_grads(left, right, out, base):
        tile = out.shape[0] // shards

        def stage_copy(i, slot):
            rows = pl.ds(pl.multiple_of(i * tile, tile), tile)
            return pltpu.make_async_copy(stage.at[slot], out.at[rows, :], stage_sems.at[slot])

        def step(i, carry):
            slot = lax.rem(i, 2)

            @pl.when(i >= 2)
            def _():
                stage_copy(i, slot).wait()

            cols = pl.ds(pl.multiple_of(i * tile, tile), tile)
            stage[slot] = dot_tn(left[:, cols], right[...]).astype(LOW)
            stage_copy(i, slot).start()
            return carry

        lax.fori_loop(0, shards, step, 0)
        for slot in range(2):
            stage_copy(slot, slot).wait()

    weight_grads(grad, act, gd_out, 0)
    for sub in range(SUBS):
        local = pl.ds(sub * swap.sub, swap.sub)
        d_hidden = swap.scatter_result(sub)
        resid = resid_ref[local, :]
        c = lax.rsqrt(jnp.mean(resid * resid, axis=-1, keepdims=True) + NORM_EPS)
        unit = resid * c
        partial = jnp.sum(d_hidden * unit, axis=0, keepdims=True)
        if sub == 0:
            gain_part_ref[...] = partial
        else:
            gain_part_ref[...] += partial
        g = d_hidden * gain_ref[...]
        d_resid = grad[swap.rows(0, sub), :].astype(F32) + c * (
            g - unit * jnp.mean(g * unit, axis=-1, keepdims=True)
        )
        d_resid_ref[local, :] = d_resid
        dest[swap.rows(0, sub), :] = d_resid.astype(LOW)
        swap.gather_start(sub)
    weight_grads(hidden, dg, gg_out, 0)
    for half, r, sub in swap.gather_steps():
        swap.gather_pass(half, r, sub)
    weight_grads(hidden, du, gu_out, 0)
    swap.scatter_end()
    swap.gather_end()
    low_copy = pltpu.make_async_copy(dest, low_out, out_sems.at[0])
    low_copy.start()
    act_copy.wait()
    low_copy.wait()


def feed(count, dp_count, hidden, d_out_low, w_gate, w_up, w_down, resid, gain):
    rows, width = hidden.shape
    units = w_gate.shape[1]
    swap = Swap(count, rows, width)
    grad_shape = jax.ShapeDtypeStruct((width, units), LOW)
    return pl.pallas_call(
        functools.partial(feed_kernel, swap, dp_count),
        out_shape=(
            jax.ShapeDtypeStruct((rows, units), LOW),
            grad_shape,
            grad_shape,
            grad_shape,
            jax.ShapeDtypeStruct((swap.block, width), F32),
            jax.ShapeDtypeStruct((rows, width), LOW),
            jax.ShapeDtypeStruct((1, width), F32),
        ),
        in_specs=[any_spec()] * 5 + [vmem_spec()] * 2,
        out_specs=(any_spec(),) * 4 + (vmem_spec(), any_spec(), vmem_spec()),
        scratch_shapes=[
            pltpu.VMEM((rows, width), LOW),
            pltpu.VMEM((rows, width), LOW),
            pltpu.VMEM((width, units), LOW),
            pltpu.VMEM((width, units), LOW),
            pltpu.VMEM((units, width), LOW),
            pltpu.VMEM((rows, units), LOW),
            pltpu.VMEM((rows, units), LOW),
            pltpu.VMEM((rows, units), LOW),
            pltpu.VMEM((rows, width), LOW),
            pltpu.VMEM((rows, width), LOW),
            pltpu.VMEM((2, width // dp_count, units), LOW),
            pltpu.SemaphoreType.DMA((5,)),
            pltpu.SemaphoreType.DMA((2,)),
            pltpu.SemaphoreType.DMA((1,)),
            *swap.scratch(),
        ],
        compiler_params=kernel_params(1),
        name="feed",
    )(hidden, d_out_low, w_gate, w_up, w_down, resid, gain[None, :])


def on_device(
    tensor_count,
    dp_count,
    tokens,
    lengths,
    in_gain,
    w_query,
    w_key,
    w_value,
    query_gain,
    key_gain,
    w_out,
    post_gain,
    w_gate,
    w_up,
    w_down,
    out_grad,
):
    row_count = tokens.shape[0]
    slot_len = row_count
    head_width = query_gain.shape[0]
    q_heads = w_query.shape[1] // head_width
    kv_heads = w_key.shape[1] // head_width
    group_size = q_heads // kv_heads
    block_len = min(512, slot_len)
    block_count = slot_len // block_len
    share = row_count // tensor_count
    score_scale = head_width ** (-0.5)
    length = lengths[0]
    tensor_me = lax.axis_index("tensor")

    def own_rows(matrix):
        return lax.dynamic_slice_in_dim(matrix, tensor_me * share, share, axis=0)

    position = jnp.arange(row_count, dtype=jnp.int32)
    valid_rows = (position < length).astype(F32)[:, None]
    inputs = tokens.astype(F32)
    normed = (unit_rows(inputs) * in_gain).astype(LOW)
    q_raw = dot_nn(normed, w_query)
    k_raw = dot_nn(normed, w_key)
    values_low = dot_nn(normed, w_value).astype(LOW).reshape(row_count, kv_heads, head_width)
    cosine, sine_table = rotary(head_width, slot_len)

    def prepare(query_in, key_in, q_gain, k_gain):
        query_heads = norm_rows(query_in.reshape(row_count, q_heads, head_width), q_gain)
        key_heads = norm_rows(key_in.reshape(row_count, kv_heads, head_width), k_gain)
        return (rotate(query_heads, cosine, sine_table), rotate(key_heads, cosine, sine_table))

    (query_rot, key_rot), prep_back = jax.vjp(prepare, q_raw, k_raw, query_gain, key_gain)
    query_low = query_rot.astype(LOW).reshape(row_count, kv_heads, group_size, head_width)
    keys_low = key_rot.astype(LOW)
    log_totals = []
    heads = []
    for block in range(block_count):
        rows = slice(block * block_len, (block + 1) * block_len)
        key_end = (block + 1) * block_len
        scores = masked_scores(
            query_low[rows], keys_low[:key_end], length, block * block_len, score_scale
        )
        row_peak = jnp.max(scores, axis=-1, keepdims=True)
        exponent = jnp.exp(scores - row_peak)
        row_total = jnp.sum(exponent, axis=-1, keepdims=True)
        probs_low = (exponent / row_total).astype(LOW)
        head_blk = (
            jnp.einsum("cgqk,kcd->qcgd", probs_low, values_low[:key_end], preferred_element_type=F32)
            .reshape(block_len, q_heads * head_width)
            .astype(LOW)
        )
        log_totals.append(row_peak + jnp.log(row_total))
        heads.append(head_blk)
    heads_low = jnp.concatenate(heads, axis=0)
    resid, hidden = out_sum(tensor_count, heads_low, w_out, own_rows(tokens), post_gain)
    d_out_low = (out_grad.astype(F32) * valid_rows).astype(LOW)
    act, grad_gate, grad_up, grad_down, d_resid, resid_low, post_gain_part = feed(
        tensor_count, dp_count, hidden, d_out_low, w_gate, w_up, w_down, resid, post_gain
    )
    mixed = lax.psum(dot_nn(act, w_down).astype(LOW), "tensor")
    resid_all = lax.all_gather(resid.astype(LOW), "tensor", tiled=True).astype(F32)
    output = (valid_rows * (resid_all + mixed.astype(F32))).astype(LOW)

    def over_dp(grad):
        return lax.psum_scatter(grad, "dp", scatter_dimension=0, tiled=True).astype(F32)

    grad_down = over_dp(grad_down).T
    grad_gate = over_dp(grad_gate)
    grad_up = over_dp(grad_up)
    q_pieces = [None] * block_count
    key_acc = jnp.zeros((slot_len, kv_heads, head_width), F32)
    value_acc = jnp.zeros((slot_len, kv_heads, head_width), F32)
    d_heads = dot_nt(resid_low, w_out).astype(LOW).reshape(row_count, kv_heads, group_size, head_width)
    for block in range(block_count):
        rows = slice(block * block_len, (block + 1) * block_len)
        key_end = (block + 1) * block_len
        query_blk = query_low[rows]
        key_blk = keys_low[:key_end]
        value_blk = values_low[:key_end]
        grad_blk = d_heads[rows]
        scores = masked_scores(query_blk, key_blk, length, block * block_len, score_scale)
        probs = jnp.exp(scores - log_totals[block])
        probs_low = probs.astype(LOW)
        d_probs = jnp.einsum("qcgd,kcd->cgqk", grad_blk, value_blk, preferred_element_type=F32)
        row_delta = jnp.sum(probs * d_probs, axis=-1, keepdims=True)
        d_scores = (probs * (d_probs - row_delta)).astype(LOW)
        q_pieces[block] = (
            jnp.einsum("cgqk,kcd->qcgd", d_scores, key_blk, preferred_element_type=F32)
            * score_scale
        )
        key_acc = key_acc.at[:key_end].add(
            jnp.einsum("cgqk,qcgd->kcd", d_scores, query_blk, preferred_element_type=F32)
            * score_scale
        )
        value_acc = value_acc.at[:key_end].add(
            jnp.einsum("cgqk,qcgd->kcd", probs_low, grad_blk, preferred_element_type=F32)
        )
    d_query_rot = jnp.concatenate(q_pieces, axis=0).reshape(row_count, q_heads, head_width)
    d_value = value_acc.reshape(row_count, kv_heads * head_width).astype(LOW)
    d_q_raw, d_k_raw, query_gain_part, key_gain_part = prep_back((d_query_rot, key_acc))
    d_query = d_q_raw.astype(LOW).reshape(row_count, -1)
    d_key = d_k_raw.astype(LOW).reshape(row_count, -1)
    normed_part = (
        dot_nt(d_query, w_query) + dot_nt(d_key, w_key) + dot_nt(d_value, w_value)
    ).astype(LOW)
    d_normed = own_rows(lax.psum(normed_part, "tensor")).astype(F32)
    in_unit, in_back = jax.vjp(unit_rows, own_rows(tokens).astype(F32))
    in_gain_part = jnp.sum(d_normed * in_unit, axis=0)
    in_rows = (d_resid + in_back(d_normed * in_gain)[0]).astype(LOW)
    in_grad = lax.all_gather(in_rows, "tensor", tiled=True)
    grad_out = over_dp(dot_tn(resid_low, heads_low).astype(LOW)).T
    grad_query = over_dp(dot_tn(normed, d_query).astype(LOW))
    grad_key = over_dp(dot_tn(normed, d_key).astype(LOW))
    grad_value = over_dp(dot_tn(normed, d_value).astype(LOW))
    grad_in_gain, grad_query_gain, grad_key_gain, grad_post_gain = lax.psum(
        (in_gain_part, query_gain_part, key_gain_part, post_gain_part[0]), ("dp", "tensor")
    )
    return (
        output,
        in_grad,
        grad_in_gain,
        grad_query,
        grad_key,
        grad_value,
        grad_query_gain,
        grad_key_gain,
        grad_out,
        grad_post_gain,
        grad_gate,
        grad_up,
        grad_down,
    )


def solution(mesh):
    tensor_count, dp_count = mesh.shape["tensor"], mesh.shape["dp"]

    def layer(*args):
        return on_device(tensor_count, dp_count, *args)

    return jax.shard_map(
        layer,
        mesh=mesh,
        in_specs=(
            P("dp", None),
            P("dp"),
            P(),
            P(None, "tensor"),
            P(None, "tensor"),
            P(None, "tensor"),
            P(),
            P(),
            P("tensor", None),
            P(),
            P(None, "tensor"),
            P(None, "tensor"),
            P("tensor", None),
            P("dp", None),
        ),
        out_specs=(
            P("dp", None),
            P("dp", None),
            P(),
            P("dp", "tensor"),
            P("dp", "tensor"),
            P("dp", "tensor"),
            P(),
            P(),
            P("tensor", "dp"),
            P(),
            P("dp", "tensor"),
            P("dp", "tensor"),
            P("tensor", "dp"),
        ),
        check_vma=False,
    )
```

time: 924 us -> 675 us (0.73)
  waiting for transfers between devices: 578 us -> 260 us
  Pallas kernels: 0 us -> 189 us
  matrix products: 171 us -> 74.8 us
  other arithmetic: 89 us -> 57.4 us
    psum x3 -> x1, waiting for transfers between devices: 383 us -> 145 us  [on_device(): mixed = lax.psum(dot_nn(act, w_down).astype(LOW), 'tensor')]
    pallas_call x0 -> x2, Pallas kernels: none -> 189 us  [the longest x1 109 us: feed(): pl.pallas_call(functools.partial(feed_kernel, swap, dp_count), out_shape=...]
    dot_general x27 -> x18, matrix products: 159 us -> 66.7 us  [the longest x4 22.7 us: dot_tn(): lax.dot_general(left, right, (((0,), (0,)), ((), ())), preferred_element_...]
    reduce_scatter x7, waiting for transfers between devices: 194 us -> 111 us  [over_dp(): lax.psum_scatter(grad, 'dp', scatter_dimension=0, tiled=True).astype(F32)]
    convert_element_type x15, other arithmetic: 47.6 us -> 32.7 us  [the longest x5 10 us: over_dp(): lax.psum_scatter(grad, 'dp', scatter_dimension=0, tiled=True).astype(F32)]
    reduce_sum x2 -> x1, other arithmetic: 16.4 us -> 2.26 us  [on_device(): in_gain_part = jnp.sum(d_normed * in_unit, axis=0)]
  transfers between devices with their start and end apart: 10 -> 10, of which waited for: 7 -> 4; matrix products, arithmetic and copies ran while one was open for 12% -> 8% of each run, Pallas kernels for 0% -> 0%
where the time goes in v1:
time: 675 us; the launch traced here: 665 us
  waiting for transfers between devices  260 us (39%)
  Pallas kernels  189 us (28%)
  matrix products  74.8 us (11%)
  other arithmetic  57.4 us (9%)
  blocking collectives  41.6 us (6%)
  local copies, waits for them, and re-layouts  23.8 us (4%)
  between operations  17.2 us (3%)
    psum x1, waiting for transfers between devices, on_device(): mixed = lax.psum(dot_nn(act, w_down).astype(LOW), 'tensor')  145 us
    reduce_scatter x7, waiting for transfers between devices, over_dp(): lax.psum_scatter(grad, 'dp', scatter_dimension=0, tiled=True).astype(F32)  111 us
    pallas_call x1, Pallas kernels, feed(): pl.pallas_call(functools.partial(feed_kernel, swap, dp_count), out_shape=...  109 us
    pallas_call x1, Pallas kernels, out_sum(): pl.pallas_call(functools.partial(out_kernel, swap), out_shape=(jax.ShapeD...  80 us
    psum x1, blocking collectives, on_device(): lax.psum((in_gain_part, query_gain_part, key_gain_part, post_gain_part[0]...  41.6 us
    dot_general x4, matrix products, dot_tn(): lax.dot_general(left, right, (((0,), (0,)), ((), ())), preferred_element_...  22.7 us
    dot_general x4, matrix products, dot_nn(): return jnp.dot(left, right, preferred_element_type=F32)  18.2 us
    unnamed x93, local copies, waits for them, and re-layouts  15.7 us
  transfers between devices with their start and end apart: 10, of which 4 were waited for; matrix products, arithmetic and copies ran while one was open for 8% of the time, Pallas kernels for 0%

profile of v1, /device:TPU:0, one launch (start us, length us, event | category | flops | bytes accessed | tf_op | source)
XLA Modules:
  0.0 664.9 jit_solution(17799136436642751739)
XLA Ops:
  8.1 3.2 fusion
  11.6 1.0 fusion.2
  12.7 3.8 multiply_reduce_fusion.2
  16.5 1.9 fusion.54
  18.6 0.9 copy.58
  19.5 4.8 multiply_reduce_fusion.5
  24.3 1.6 copy.56
  26.2 1.8 subtract_convert_fusion.1
  29.0 1.3 convolution_convert_fusion.6
  31.9 0.9 fusion.52
  32.8 1.2 fusion.69
  34.6 1.8 fusion.43
  36.4 2.1 copy.110
  38.9 3.2 fusion.68
  42.1 1.2 fusion.6
  43.3 2.1 copy-done.1
  45.4 2.4 fusion.44
  47.8 2.1 copy.111
  49.9 2.5 fusion.24
  52.5 2.2 pad_maximum_fusion.1.heads_ref
  54.7 2.8 multiply_convert_fusion.1.grad_hbm
  57.5 80.0 %out_sum.1 = (f32[256,2048]{1,0:T(8,128)}, bf16[1024,2048]{1,0:T(8,128)(2,1)}) custom-call(bf16[1024,512]{1,0:T(8,128)(2,1)} %pad_maximum_fusion.1.heads_ref, bf16[512,2048]{1,0:T(8,128)(2,1)} %w_ref.1, bf16[256,2048]{1,0:T(8,128)(2,1)} %get-tuple-element.134.x_ref, f32[1,2048]{1,0:T(1,128)} %bitcast.199), custom_call_target="tpu_custom_call" | custom-call | tf_op jit(solution)/shard_map/out_sum/pallas_call | solution.py:300
  137.4 109.2 %feed.1 = (bf16[1024,1536]{1,0:T(8,128)(2,1)}, bf16[2048,1536]{1,0:T(8,128)(2,1)}, bf16[2048,1536]{1,0:T(8,128)(2,1)}, bf16[2048,1536]{1,0:T(8,128)(2,1)}, f32[2...) custom-call(bf16[1024,2048]{1,0:T(8,128)(2,1)} %get-tuple-element.87.hidden_hbm, ...), custom_call_target="tpu_custom_call" | custom-call | tf_op jit(solution)/shard_map/feed/pallas_call | solution.py:456
  246.7 5.4 convolution_convert_fusion.5
  252.2 0.8 fusion.47
  253.0 0.9 fusion.10
  254.0 1.2 fusion.12
  256.0 1.5 fusion.36
  258.5 2.0 fusion.3
  260.5 2.4 fusion.40
  262.9 2.4 fusion.5
  265.3 2.0 fusion.35
  267.3 1.2 fusion.34
  269.0 0.9 multiply_reduce_fusion.3
  270.0 1.7 fusion.50
  271.7 1.2 copy.81
  273.0 2.7 fusion.71
  278.8 2.4 fusion.70
  281.5 0.9 copy-done.40
  282.4 8.4 %convolution_convert_fusion = bf16[1024,2048]{1,0:T(8,128)(2,1)} fusion(bf16[1024,1536]{1,0:T(8,128)(2,1)S(1)} %copy-done.40, bf16[1536,2048]{1,0:T(8,128)(2,1)S(1)} %bitcast.177), kind=kOutput, calls=%fused_computation.31 | convolution fusion | flops 6444548096 | bytes 13631488 | tf_op jit(solution)/shard_map/dot_general | solution.py:51
  290.8 3.3 add_convert_fusion
  294.2 4.5 convolution_convert_fusion.3
  298.8 5.5 convolution_convert_fusion.4
  304.4 6.1 convolution_convert_fusion.1
  310.6 6.6 convolution_convert_fusion.2
  317.2 2.7 convert_element_type.149
  322.4 144.8 %all-reduce.10.cloned.1.call-done = (bf16[1024,2048]{1,0:T(8,128)(2,1)}, bf16[1024,2048]{1,0:T(8,128)(2,1)}) async-done(((bf16[1024,2048]{1,0:T(8,128)(2,1)}, bf16[1024,2048]{1,0:T(8,128)(2,1)}), (bf16[1024,2048]{1,0:T(8,128)(2,1)}, bf16[1024,2048]{1,0:T(8,128)(2,1)})) %all-reduce.10.cloned.1.call-update) | async-done | bytes 8388624 | tf_op jit(solution)/shard_map/psum | solution.py:567
  467.2 2.3 fusion.18
  469.5 3.5 fusion.21
  473.1 1.6 convert_element_type.176
  474.7 1.6 convert_element_type.174
  476.4 1.0 convert_bitcast_fusion.1
  477.4 1.0 copy.84
  478.4 1.8 convert_element_type.172
  480.3 41.6 %all-reduce.6 = (f32[2048]{0:T(1024)}, f32[128]{0:T(128)}, f32[128]{0:T(128)}, f32[2048]{0:T(1024)}) all-reduce(f32[2048]{0:T(1024)S(1)} %get-tuple-element.121, f32[128]{0:T(128)S(1)} %get-tuple-element.125, f32[128]{0:T(128)S(1)} %get-tuple-element.123, f32[2048]{0:T(1024)S(1)} %bitcast.201), channel_id=1, replica_groups=mesh['dp'=8,'tensor'=4] {'dp','tensor'}, use_global_device_ids=true, to_apply=%region_16.17 | all-reduce | flops 4352 | bytes 34816 | tf_op jit(solution)/shard_map/psum | solution.py:622
  521.8 2.7 all-gather.3.cloned.1.call-done
  524.5 6.8 %multiply_convert_fusion = bf16[1024,2048]{1,0:T(8,128)(2,1)} fusion(bf16[1024,2048]{1,0:T(8,128)(2,1)} %get-tuple-element.131, bf16[1024,2048]{1,0:T(8,128)(2,1)} %all-gather.3.cloned.1.call-done, f32[1024]{0:T(1024)S(1)} %fusion.62), kind=kLoop, calls=%fused_computation.13 | loop fusion | flops 10485760 | bytes 12587008 | tf_op jit(solution)/shard_map/convert_element_type | solution.py:569
  531.3 2.5 convert_bitcast_fusion
  533.8 3.2 copy.85
  537.1 42.6 %reduce-scatter.16.cloned.1.call-done = bf16[256,1536]{1,0:T(8,128)(2,1)} async-done(((bf16[2048,1536]{1,0:T(8,128)(2,1)}), bf16[256,1536]{1,0:T(8,128)(2,1)}) %reduce-scatter.16.cloned.1.call-update) | async-done | bytes 786448 | tf_op jit(solution)/shard_map/reduce_scatter | solution.py:572
  579.7 2.5 convert_element_type.178
  582.1 67.9 %reduce-scatter.18.cloned.1.call-done = bf16[256,1536]{1,0:T(8,128)(2,1)} async-done(((bf16[2048,1536]{1,0:T(8,128)(2,1)}), bf16[256,1536]{1,0:T(8,128)(2,1)}) %reduce-scatter.18.cloned.1.call-update) | async-done | bytes 786448 | tf_op jit(solution)/shard_map/reduce_scatter | solution.py:572
  650.1 2.5 convert_element_type.179
  652.5 4.8 copy.130
  (145 shorter events, 12.1 us)
Async XLA Ops:
  8.0 4.7 copy-start
  8.0 3.3 copy-start.36
  8.0 459.2 %all-reduce.10.cloned.1.call-start = ((), (), s32[]{:S(2)}) async-start(), calls=%async_computation.16 | async-start | bytes 16777216 | tf_op jit(solution)/shard_map/psum | solution.py:567
  8.1 3.6 copy-start.6
  12.7 3.8 copy-start.18
  18.4 5.9 copy-start.8
  18.4 5.9 copy-start.10
  19.5 6.4 copy-start.38
  25.9 3.1 copy-start.19
  25.9 3.1 copy-start.31
  28.1 4.7 copy-start.12
  28.1 4.7 copy-start.14
  29.0 1.6 copy-start.4
  29.0 1.6 copy-start.39
  30.3 1.6 copy-start.28
  30.3 1.2 copy-start.23
  30.3 4.3 copy-start.33
  32.7 1.9 copy-start.16
  34.0 2.4 copy-start.2
  42.1 3.3 copy-start.1
  42.1 3.3 copy-start.29
  49.9 4.8 copy-start.20
  246.7 5.5 copy-start.3
  252.1 1.0 copy-start.34
  254.0 3.6 slice-start
  254.0 1.3 copy-start.17
  254.0 2.0 copy-start.13
  254.0 2.0 copy-start.15
  254.0 4.3 slice-start.1
  255.2 3.3 copy-start.30
  265.3 2.0 copy-start.26
  267.3 1.3 copy-start.9
  267.3 1.3 copy-start.11
  272.9 2.7 copy-start.21
  272.9 2.7 copy-start.22
  275.7 1.0 copy-start.24
  275.7 1.7 copy-start.5
  278.2 3.0 slice-start.2
  278.8 2.4 copy-start.35
  278.8 2.7 slice-start.3
  278.8 3.6 copy-start.40
  282.4 8.4 %copy-start.25 = (bf16[1024,2,128]{0,2,1:T(8,128)(2,1)S(1)}, bf16[1024,2,128]{0,2,1:T(8,128)(2,1)}, u32[]{:S(2)}) copy-start(bf16[1024,2,128]{0,2,1:T(8,128)(2,1)} %fusion.40) | copy-start | bytes 1572868
  282.4 8.4 %copy-start.32 = (bf16[2048,256]{1,0:T(8,128)(2,1)S(1)}, bf16[2048,256]{1,0:T(8,128)(2,1)}, u32[]{:S(2)}) copy-start(bf16[2048,256]{1,0:T(8,128)(2,1)} %param.31) | copy-start | bytes 3145732
  294.2 178.9 %reduce-scatter.12.cloned.1.call-start = ((), (), s32[]{:S(2)}) async-start(), calls=%async_computation.11 | async-start | bytes 1179648 | tf_op jit(solution)/shard_map/reduce_scatter | solution.py:572
  298.7 5.6 copy-start.27
  298.8 176.0 %reduce-scatter.10.cloned.1.call-start = ((), (), s32[]{:S(2)}) async-start(), calls=%async_computation.10 | async-start | bytes 1179648 | tf_op jit(solution)/shard_map/reduce_scatter | solution.py:572
  304.3 172.1 %reduce-scatter.14.cloned.1.call-start = ((), (), s32[]{:S(2)}) async-start(), calls=%async_computation.12 | async-start | bytes 2359296 | tf_op jit(solution)/shard_map/reduce_scatter | solution.py:572
  310.5 167.9 %reduce-scatter.8.cloned.1.call-start = ((), (), s32[]{:S(2)}) async-start(), calls=%async_computation.9 | async-start | bytes 2359296 | tf_op jit(solution)/shard_map/reduce_scatter | solution.py:572
  317.2 207.3 %all-gather.3.cloned.1.call-start = ((), (), s32[]{:S(2)}) async-start(), calls=%async_computation.7 | async-start | bytes 5242880 | tf_op jit(solution)/shard_map/all_gather | solution.py:568
  320.0 211.4 %reduce-scatter.20.cloned.1.call-start = ((), (), s32[]{:S(2)}) async-start(), calls=%async_computation.15 | async-start | bytes 7077888 | tf_op jit(solution)/shard_map/reduce_scatter | solution.py:572
  320.7 258.9 %reduce-scatter.16.cloned.1.call-start = ((), (), s32[]{:S(2)}) async-start(), calls=%async_computation.13 | async-start | bytes 7077888 | tf_op jit(solution)/shard_map/reduce_scatter | solution.py:572
  321.5 145.8 %copy-start.7 = (bf16[256,2048]{1,0:T(8,128)(2,1)S(1)}, bf16[256,2048]{1,0:T(8,128)(2,1)}, u32[]{:S(2)}) copy-start(bf16[256,2048]{1,0:T(8,128)(2,1)} %get-tuple-element.134.x_ref) | copy-start | bytes 3145732
  321.5 328.6 %reduce-scatter.18.cloned.1.call-start = ((), (), s32[]{:S(2)}) async-start(), calls=%async_computation.14 | async-start | bytes 7077888 | tf_op jit(solution)/shard_map/reduce_scatter | solution.py:572
  322.1 330.4 %all-gather.5.cloned.1.call-start = ((), (), s32[]{:S(2)}) async-start(), calls=%async_computation.8 | async-start | bytes 5242880 | tf_op jit(solution)/shard_map/all_gather | solution.py:617
  469.5 10.7 %copy-start.37 = (f32[1,2048]{1,0:T(1,128)S(1)}, f32[1,2048]{1,0:T(1,128)}, u32[]{:S(2)}) copy-start(f32[1,2048]{1,0:T(1,128)} %get-tuple-element.91) | copy-start | bytes 24580
Sparse Core Ops, SparseCore 0:
  294.3 172.9 all-reduce.9
  469.8 54.6 all-gather.2
  527.1 52.6 all-gather.4
Sparse Core Ops, SparseCore 1:
  298.8 32.6 reduce-scatter.11
  334.3 30.6 reduce-scatter.9
  367.2 33.6 reduce-scatter.13
  403.3 34.3 reduce-scatter.7
  440.1 69.0 reduce-scatter.19
  511.6 68.0 reduce-scatter.15
  582.0 68.0 reduce-scatter.17

commit v2 on v1

v2 whole, which is shorter than its diff:
```python
import functools

import jax
import jax.numpy as jnp
from jax import lax
from jax.experimental import pallas as pl
from jax.experimental.pallas import tpu as pltpu
from jax.sharding import PartitionSpec as P

NORM_EPS = 1e-06
ROPE_BASE = 1000000.0
MASK_FILL = -1e30
LOW = jnp.bfloat16
F32 = jnp.float32
MESH = pl.DeviceIdType.MESH
VMEM_BYTES = 63 * 1024 * 1024
SUBS = 2


def unit_rows(matrix):
    return matrix * lax.rsqrt(jnp.mean(matrix * matrix, axis=-1, keepdims=True) + NORM_EPS)


def norm_rows(matrix, scale_gain):
    return unit_rows(matrix) * scale_gain


def rotary(head_width, row_count):
    half_width = head_width // 2
    inv_freq = ROPE_BASE ** (-2.0 * jnp.arange(half_width, dtype=F32) / head_width)
    angles = jnp.arange(row_count, dtype=F32)[:, None] * inv_freq[None, :]
    return (jnp.cos(angles), jnp.sin(angles))


def rotate(matrix, cosine, sine_table):
    half_width = matrix.shape[-1] // 2
    first_half = matrix[..., :half_width]
    second_half = matrix[..., half_width:]
    cos_part = cosine[:, None, :]
    sin_part = sine_table[:, None, :]
    return jnp.concatenate(
        [
            first_half * cos_part - second_half * sin_part,
            second_half * cos_part + first_half * sin_part,
        ],
        axis=-1,
    )


def dot_nn(left, right):
    return jnp.dot(left, right, preferred_element_type=F32)


def dot_tn(left, right):
    return lax.dot_general(left, right, (((0,), (0,)), ((), ())), preferred_element_type=F32)


def dot_nt(left, right):
    return lax.dot_general(left, right, (((1,), (1,)), ((), ())), preferred_element_type=F32)


def masked_scores(query_blk, key_blk, length, offset, score_scale):
    scores = (
        jnp.einsum("qcgd,kcd->cgqk", query_blk, key_blk, preferred_element_type=F32) * score_scale
    )
    q_pos = offset + jnp.arange(query_blk.shape[0], dtype=jnp.int32)
    k_pos = jnp.arange(key_blk.shape[0], dtype=jnp.int32)
    allowed = (k_pos[None, :] <= q_pos[:, None]) & (k_pos[None, :] < length)
    return jnp.where(allowed, scores, MASK_FILL)


class Swap:
    def __init__(self, count, rows, width):
        self.count, self.width = count, width
        self.bits = count.bit_length() - 1
        self.block = rows // count
        self.sub = self.block // SUBS
        self.half = width // 2
        self.orders = [list(range(self.bits)), list(range(self.bits))[::-1]]
        self.slots = []
        for order in self.orders:
            slot = {}
            for step in range(self.bits):
                for r in range(count):
                    if not any(r >> b & 1 for b in order[: step + 1]):
                        slot[step, r] = len(slot)
            self.slots.append(slot)

    def landing(self):
        return pltpu.VMEM((2, self.count - 1, self.block, self.half), LOW)

    def semaphores(self):
        n = self.count
        return [
            pltpu.SemaphoreType.DMA((2, n, SUBS)),
            pltpu.SemaphoreType.DMA((2, n, SUBS)),
            pltpu.SemaphoreType.DMA((2, n * self.bits, SUBS)),
            pltpu.SemaphoreType.DMA((2, n, SUBS)),
        ]

    def bind(self, part, recv, dest, sems, own=None):
        self.part, self.recv, self.dest, self.sems = part, recv, dest, sems
        self.own = dest if own is None else own
        self.me = lax.axis_index("tensor")
        return self

    def near(self, bit):
        own = (self.me // 2**bit) % 2
        return self.me + (1 - 2 * own) * 2**bit

    def rows(self, r, sub=None):
        owner = self.me
        for bit in range(self.bits):
            if r >> bit & 1:
                own = (self.me // 2**bit) % 2
                owner = owner + (1 - 2 * own) * 2**bit
        start = owner * self.block
        if sub is None:
            return pl.ds(pl.multiple_of(start, self.block), self.block)
        return pl.ds(pl.multiple_of(start + sub * self.sub, self.sub), self.sub)

    def columns(self, half):
        return pl.ds(half * self.half, self.half)

    def signal(self, sem):
        for bit in range(self.bits):
            pl.semaphore_signal(
                sem, inc=1, device_id={"tensor": self.near(bit)}, device_id_type=MESH
            )

    def first(self, half, r):
        return next(k for k, bit in enumerate(self.orders[half]) if r >> bit & 1)

    def scatter_copy(self, half, r, sub):
        step = self.first(half, r)
        bit = self.orders[half][step]
        slot = self.slots[half][step, r ^ (1 << bit)]
        return pltpu.make_async_remote_copy(
            src_ref=self.part.at[self.rows(r, sub), self.columns(half)],
            dst_ref=self.recv.at[half, slot, pl.ds(sub * self.sub, self.sub)],
            send_sem=self.sems[0].at[half, r, sub],
            recv_sem=self.sems[1].at[half, slot, sub],
            device_id={"tensor": self.near(bit)},
            device_id_type=MESH,
        )

    def scatter_wait(self, half, step, r, sub):
        slot = self.slots[half][step, r]
        ref = self.recv.at[half, slot, pl.ds(sub * self.sub, self.sub)]
        pltpu.make_async_copy(ref, ref, self.sems[1].at[half, slot, sub]).wait()
        return ref

    def scatter_start(self, r):
        for sub in range(SUBS):
            for half in range(2):
                if self.first(half, r) == 0:
                    self.scatter_copy(half, r, sub).start()

    def scatter_forward(self, half, r):
        step = self.first(half, r)
        for sub in range(SUBS):
            where = self.rows(r, sub), self.columns(half)
            total = self.part[where].astype(F32)
            for j in range(step):
                total = total + self.scatter_wait(half, j, r, sub)[...].astype(F32)
            self.part[where] = total.astype(LOW)
            self.scatter_copy(half, r, sub).start()

    def forwards(self):
        todo = [
            (self.first(half, r), half, r)
            for half in range(2)
            for r in range(1, self.count)
            if self.first(half, r) > 0
        ]
        return [(half, r) for _, half, r in sorted(todo)]

    def scatter_result(self, sub):
        total = []
        for half in range(2):
            value = self.part[self.rows(0, sub), self.columns(half)].astype(F32)
            for j in range(self.bits):
                value = value + self.scatter_wait(half, j, 0, sub)[...].astype(F32)
            total.append(value)
        return jnp.concatenate(total, axis=1)

    def scatter_end(self):
        for half in range(2):
            for r in range(1, self.count):
                for sub in range(SUBS):
                    self.scatter_copy(half, r, sub).wait_send()

    def last(self, half, r):
        order = self.orders[half][::-1]
        return max([-1] + [j for j, bit in enumerate(order) if r >> bit & 1])

    def gather_copy(self, half, r, step, sub):
        bit = self.orders[half][::-1][step]
        where = self.rows(r, sub), self.columns(half)
        return pltpu.make_async_remote_copy(
            src_ref=self.dest.at[where] if r else self.own.at[where],
            dst_ref=self.dest.at[where],
            send_sem=self.sems[2].at[half, r * self.bits + step, sub],
            recv_sem=self.sems[3].at[half, r ^ (1 << bit), sub],
            device_id={"tensor": self.near(bit)},
            device_id_type=MESH,
        )

    def gather_start(self, sub):
        for step in range(self.bits):
            for half in range(2):
                self.gather_copy(half, 0, step, sub).start()

    def gather_wait(self, half, r, sub):
        ref = self.dest.at[self.rows(r, sub), self.columns(half)]
        pltpu.make_async_copy(ref, ref, self.sems[3].at[half, r, sub]).wait()

    def gather_steps(self):
        todo = [
            (self.last(half, r), sub, bin(r).count("1"), half, r)
            for half in range(2)
            for r in range(1, self.count)
            for sub in range(SUBS)
        ]
        return [(half, r, sub) for _, sub, _, half, r in sorted(todo)]

    def gather_pass(self, half, r, sub):
        self.gather_wait(half, r, sub)
        for step in range(self.last(half, r) + 1, self.bits):
            self.gather_copy(half, r, step, sub).start()

    def gather_early(self):
        return [it for it in self.gather_steps() if self.last(it[0], it[1]) < self.bits - 1]

    def gather_late(self):
        return [it for it in self.gather_steps() if self.last(it[0], it[1]) == self.bits - 1]

    def gather_end(self):
        for half in range(2):
            for r in range(self.count):
                for step in range(self.last(half, r) + 1, self.bits):
                    for sub in range(SUBS):
                        self.gather_copy(half, r, step, sub).wait_send()

    def order(self):
        return sorted(range(self.count), key=lambda r: (-bin(r).count("1"), r))


def tiled(total, size, body):
    count = total // size

    def step(i, carry):
        body(pl.ds(pl.multiple_of(i * size, size), size))
        return carry

    lax.fori_loop(0, count, step, 0)


def any_spec():
    return pl.BlockSpec(memory_space=pl.ANY)


def vmem_spec():
    return pl.BlockSpec(memory_space=pltpu.VMEM)


def kernel_params(identity):
    return pltpu.CompilerParams(
        collective_id=identity, has_side_effects=True, vmem_limit_bytes=VMEM_BYTES
    )


def out_kernel(
    swap, heads_ref, w_ref, x_ref, gain_ref, resid_ref, hidden_ref, part, dest, local_sem, recv, *sems
):
    swap.bind(part, recv, dest, sems)
    barrier = pltpu.get_barrier_semaphore()
    swap.signal(barrier)
    pl.semaphore_wait(barrier, swap.bits)
    for r in swap.order():
        rows = swap.rows(r)

        def columns(cols):
            part[rows, cols] = dot_nn(heads_ref[rows, :], w_ref[:, cols]).astype(LOW)

        tiled(swap.width, 512, columns)
        if r:
            swap.scatter_start(r)
    for half, r in swap.forwards():
        swap.scatter_forward(half, r)
    for sub in range(SUBS):
        local = pl.ds(sub * swap.sub, swap.sub)
        resid = x_ref[local, :].astype(F32) + swap.scatter_result(sub)
        resid_ref[local, :] = resid
        dest[swap.rows(0, sub), :] = (unit_rows(resid) * gain_ref[...]).astype(LOW)
        swap.gather_start(sub)
    for half, r, sub in swap.gather_steps():
        swap.gather_pass(half, r, sub)
    swap.scatter_end()
    swap.gather_end()
    copy = pltpu.make_async_copy(dest, hidden_ref, local_sem)
    copy.start()
    copy.wait()


def out_sum(count, heads, w_out, x_rows, gain):
    rows, width = heads.shape[0], w_out.shape[1]
    swap = Swap(count, rows, width)
    return pl.pallas_call(
        functools.partial(out_kernel, swap),
        out_shape=(
            jax.ShapeDtypeStruct((swap.block, width), F32),
            jax.ShapeDtypeStruct((rows, width), LOW),
        ),
        in_specs=[vmem_spec()] * 4,
        out_specs=(vmem_spec(), any_spec()),
        scratch_shapes=[
            pltpu.VMEM((rows, width), LOW),
            pltpu.VMEM((rows, width), LOW),
            pltpu.SemaphoreType.DMA,
            swap.landing(),
            *swap.semaphores(),
        ],
        compiler_params=kernel_params(0),
        name="out_sum",
    )(heads, w_out, x_rows, gain[None, :])


class Line:
    def __init__(self, count, groups, tile, width):
        self.count, self.groups, self.tile, self.width = count, groups, tile, width
        self.places = count // 2

    def outputs(self):
        shape = (self.tile, self.width)
        return [
            jax.ShapeDtypeStruct((self.groups, self.places) + shape, LOW),
            jax.ShapeDtypeStruct((self.groups, self.places) + shape, LOW),
            jax.ShapeDtypeStruct((self.groups, self.places + 1) + shape, LOW),
        ]

    def semaphores(self):
        g, n = self.groups, self.places
        return [
            pltpu.SemaphoreType.DMA((g, n)),
            pltpu.SemaphoreType.DMA((g, n)),
            pltpu.SemaphoreType.DMA((2,)),
            pltpu.SemaphoreType.DMA((2, g, n)),
            pltpu.SemaphoreType.DMA((g, n + 1)),
            pltpu.SemaphoreType.DMA((6,)),
        ]

    def bind(self, core_land, acc, land, stage, extra, sems):
        self.core_land, self.acc, self.land = core_land, acc, land
        self.stage, self.extra = stage, extra
        (
            self.core_send,
            self.core_recv,
            self.stage_sem,
            self.line_send,
            self.line_recv,
            self.local_sem,
        ) = sems
        self.me = lax.axis_index("dp")
        self.place = self.me // 2
        self.core = self.me % 2
        self.other = self.me + 1 - 2 * self.core
        self.before = []
        return self

    def signal(self, sem):
        pl.semaphore_signal(sem, inc=1, device_id={"dp": self.other}, device_id_type=MESH)

        @pl.when(self.place > 0)
        def _():
            pl.semaphore_signal(sem, inc=1, device_id={"dp": self.me - 2}, device_id_type=MESH)

        @pl.when(self.place < self.places - 1)
        def _():
            pl.semaphore_signal(sem, inc=1, device_id={"dp": self.me + 2}, device_id_type=MESH)

    def peers(self):
        ends = (self.places - 1 - self.place) // (self.places - 1) + self.place // (self.places - 1)
        return 3 - ends

    def core_copy(self, group, i, slot):
        return pltpu.make_async_remote_copy(
            src_ref=self.stage.at[slot],
            dst_ref=self.core_land.at[group, i],
            send_sem=self.core_send.at[group, i],
            recv_sem=self.core_recv.at[group, i],
            device_id={"dp": self.other},
            device_id_type=MESH,
        )

    def fill(self, group, tile_of):
        def away(i, carry):
            slot = lax.rem(i, 2)

            @pl.when(i >= 2)
            def _():
                self.core_copy(group, i - 2, slot).wait_send()

            self.stage[slot] = tile_of(2 * i + 1 - self.core).astype(LOW)
            self.core_copy(group, i, slot).start()
            return carry

        lax.fori_loop(0, self.places, away, 0)
        for i in range(max(0, self.places - 2), self.places):
            self.core_copy(group, i, i % 2).wait_send()

        def store(i, slot):
            return pltpu.make_async_copy(
                self.stage.at[slot], self.acc.at[group, i], self.stage_sem.at[slot]
            )

        def home(i, carry):
            slot = lax.rem(i, 2)
            landed = self.core_land.at[group, i]
            pltpu.make_async_copy(landed, landed, self.core_recv.at[group, i]).wait()
            fetch = pltpu.make_async_copy(landed, self.extra, self.local_sem.at[0])
            fetch.start()

            @pl.when(i >= 2)
            def _():
                store(i - 2, slot).wait()

            value = tile_of(2 * i + self.core)
            fetch.wait()
            self.stage[slot] = (value + self.extra[...].astype(F32)).astype(LOW)
            store(i, slot).start()
            return carry

        lax.fori_loop(0, self.places, home, 0)
        for i in range(max(0, self.places - 2), self.places):
            store(i, i % 2).wait()
        self.ends(group, "start")

    def line_copy(self, group, way, j, source):
        if way == 0:
            slot, to = j, self.me + 2
        else:
            final = 1 - jnp.minimum(self.place - 1 - j, 1)
            slot, to = j + final * (self.places - j), self.me - 2
        return pltpu.make_async_remote_copy(
            src_ref=source,
            dst_ref=self.land.at[group, slot],
            send_sem=self.line_send.at[way, group, j],
            recv_sem=self.line_recv.at[group, slot],
            device_id={"dp": to},
            device_id_type=MESH,
        )

    def ends(self, group, act):
        n = self.places

        @pl.when(self.place == 0)
        def _():
            for j in range(n - 1, 0, -1):
                copy = self.line_copy(group, 0, j, self.acc.at[group, j])
                copy.start() if act == "start" else copy.wait_send()

        @pl.when(self.place == n - 1)
        def _():
            for j in range(n - 1):
                copy = self.line_copy(group, 1, j, self.acc.at[group, j])
                copy.start() if act == "start" else copy.wait_send()

    def landed(self, group, slot):
        ref = self.land.at[group, slot]
        pltpu.make_async_copy(ref, ref, self.line_recv.at[group, slot]).wait()
        return ref

    def on_way(self, step, way):
        far = self.place if way == 0 else self.places - 1 - self.place
        index = self.places - 1 - step + self.place if way == 0 else step - far
        return jnp.logical_and(far >= 1, far <= step), index

    def settle(self, lines):
        for group, step in self.before:
            for way in range(2):
                active, j = self.on_way(step, way)

                @pl.when(active)
                def _(way=way, j=j, group=group):
                    self.line_copy(group, way, j, lines.at[way, 0]).wait_send()

        self.before = []

    def tick(self, group, step, lines):
        self.settle(lines)
        for way in range(2):
            active, j = self.on_way(step, way)

            @pl.when(active)
            def _(way=way, j=j):
                here = pltpu.make_async_copy(
                    self.acc.at[group, j], lines.at[way, 0], self.local_sem.at[2 * way]
                )
                here.start()
                there = pltpu.make_async_copy(
                    self.landed(group, j), lines.at[way, 1], self.local_sem.at[2 * way + 1]
                )
                there.start()
                here.wait()
                there.wait()
                lines[way, 0] = (
                    lines[way, 0].astype(F32) + lines[way, 1].astype(F32)
                ).astype(LOW)
                self.line_copy(group, way, j, lines.at[way, 0]).start()

        self.before = [(group, step)]

    def finish(self, group, lines, total):
        self.settle(lines)
        n = self.places
        here = pltpu.make_async_copy(
            self.acc.at[group, self.place], lines.at[0, 0], self.local_sem.at[0]
        )
        here.start()
        here.wait()
        total[...] = lines[0, 0].astype(F32)

        @pl.when(self.place > 0)
        def _():
            there = pltpu.make_async_copy(
                self.landed(group, self.place), lines.at[0, 1], self.local_sem.at[1]
            )
            there.start()
            there.wait()
            total[...] += lines[0, 1].astype(F32)

        @pl.when(self.place < n - 1)
        def _():
            there = pltpu.make_async_copy(
                self.landed(group, n), lines.at[1, 1], self.local_sem.at[2]
            )
            there.start()
            there.wait()
            total[...] += lines[1, 1].astype(F32)


def head_back(grad, raw, cosine, sine, gain):
    width = raw.shape[-1]
    turned = grad * cosine - pltpu.roll(grad, width // 2, 1) * sine
    scale = lax.rsqrt(jnp.mean(raw * raw, axis=-1, keepdims=True) + NORM_EPS)
    unit = raw * scale
    gain_sum = jnp.sum(turned * unit, axis=0, keepdims=True)
    inner = turned * gain
    return scale * (inner - unit * jnp.mean(inner * unit, axis=-1, keepdims=True)), gain_sum


def rows_back(d_unit, rows, scale):
    unit = rows * scale
    return scale * (d_unit - unit * jnp.mean(d_unit * unit, axis=-1, keepdims=True))


def inverse_norm(rows):
    return lax.rsqrt(jnp.mean(rows * rows, axis=-1, keepdims=True) + NORM_EPS)


def back_kernel(plan, *refs):
    swap3, swap2, swap4, line, sizes = plan
    q_block, head_width, pairs, group_size = sizes
    refs = iter(refs)

    def take(count):
        return [next(refs) for _ in range(count)]

    (
        length_ref,
        hidden_hbm,
        grad_hbm,
        wg_hbm,
        wu_hbm,
        wd_hbm,
        resid_ref,
        post_gain_ref,
        in_gain_ref,
        query_gain_ref,
        key_gain_ref,
        valid_ref,
        lse_ref,
        x_hbm,
        q_hbm,
        k_hbm,
        v_hbm,
        heads_hbm,
        normed_hbm,
        q_raw_hbm,
        k_raw_hbm,
        cos_hbm,
        sin_hbm,
        w_out_hbm,
        w_query_hbm,
        w_key_hbm,
        w_value_hbm,
    ) = take(27)
    (
        output,
        in_grad,
        post_part,
        in_part,
        query_part,
        key_part,
        down_out,
        gate_out,
        up_out,
        query_out,
        key_out,
        value_out,
        proj_out,
        core_land,
        acc,
        land,
    ) = take(16)
    hidden, grad, act, dg, du, part, low, d_resid, stage, extra, recv = take(11)
    in_sems, own_sems, final_sems, free_sem = take(4)
    sems3, sems2, sems4 = take(4), take(4), take(4)
    swap3.bind(part, recv, low, sems3)
    swap2.bind(part, recv, output, sems2, own=part)
    swap4.bind(grad, recv, in_grad, sems4, own=grad)
    line.bind(core_land, acc, land, stage, extra, take(6))

    units = act.shape[1]
    width = swap3.width
    rows_all, heads_width = q_hbm.shape
    keys_width = k_hbm.shape[1]
    unit_tile = 512 if units % 512 == 0 else 256

    def load(i, src, dst):
        return pltpu.make_async_copy(src, dst, in_sems.at[i])

    def weights(wg, wu, wd):
        loads = [
            load(0, hidden_hbm, hidden),
            load(1, wg_hbm, wg),
            load(2, wu_hbm, wu),
            load(3, grad_hbm, grad),
            load(4, wd_hbm, wd),
        ]
        for item in loads:
            item.start()
        barrier = pltpu.get_barrier_semaphore()
        swap3.signal(barrier)
        line.signal(barrier)
        pl.semaphore_wait(barrier, swap3.bits + line.peers())
        for item in loads:
            item.wait()
        order = swap3.order()
        for spot, r in enumerate(order):
            rows = swap3.rows(r)

            def unit_step(cols):
                gate = dot_nn(hidden[rows, :], wg[:, cols])
                up = dot_nn(hidden[rows, :], wu[:, cols])
                d_act = dot_nt(grad[rows, :], wd[cols, :])
                sig = jax.nn.sigmoid(gate)
                silu = gate * sig
                act[rows, cols] = (silu * up).astype(LOW)
                dg[rows, cols] = (d_act * up * sig * (1.0 + gate * (1.0 - sig))).astype(LOW)
                du[rows, cols] = (d_act * silu).astype(LOW)

            tiled(units, unit_tile, unit_step)

            def back_step(cols):
                part[rows, cols] = (
                    dot_nt(dg[rows, :], wg[cols, :]) + dot_nt(du[rows, :], wu[cols, :])
                ).astype(LOW)

            tiled(width, 512, back_step)
            if r:
                swap3.scatter_start(r)
            if spot == len(order) - 2:
                for half, s in swap3.forwards():
                    swap3.scatter_forward(half, s)

        def tile_cols(i):
            return pl.ds(pl.multiple_of(i * line.tile, line.tile), line.tile)

        line.fill(0, lambda i: dot_tn(grad[:, tile_cols(i)], act[...]))
        for sub in range(SUBS):
            local = pl.ds(sub * swap3.sub, swap3.sub)
            d_hidden = swap3.scatter_result(sub)
            resid = resid_ref[local, :]
            c = inverse_norm(resid)
            partial = jnp.sum(d_hidden * (resid * c), axis=0, keepdims=True)
            if sub == 0:
                post_part[...] = partial
            else:
                post_part[...] += partial
            value = grad[swap3.rows(0, sub), :].astype(F32) + rows_back(
                d_hidden * post_gain_ref[...], resid, c
            )
            d_resid[local, :] = value
            low[swap3.rows(0, sub), :] = value.astype(LOW)
            swap3.gather_start(sub)
        swap3.scatter_end()
        early = swap3.gather_early()
        for spot, r in enumerate(order):
            rows = swap3.rows(r)

            def mix_step(cols):
                part[rows, cols] = dot_nn(act[rows, :], wd[:, cols]).astype(LOW)

            tiled(width, 512, mix_step)
            if spot == 1:
                for item in early[: len(early) // 2]:
                    swap3.gather_pass(*item)
        for item in early[len(early) // 2 :]:
            swap3.gather_pass(*item)

    def rest(lines, total, turned, w_out, w_query, w_key, w_value, q_raw, k_raw, cosine, sine, dk, dv):
        def tile_cols(i):
            return pl.ds(pl.multiple_of(i * line.tile, line.tile), line.tile)

        loads = [
            load(5, w_out_hbm, w_out),
            load(6, w_query_hbm, w_query),
            load(7, w_key_hbm, w_key),
            load(8, w_value_hbm, w_value),
            load(9, q_raw_hbm, q_raw),
            load(10, k_raw_hbm, k_raw),
            load(11, cos_hbm, cosine),
            load(12, sin_hbm, sine),
        ]
        q_at = pl.ds(0, heads_width)
        k_at = pl.ds(heads_width, keys_width)
        v_at = pl.ds(heads_width + keys_width, keys_width)
        o_at = pl.ds(heads_width + 2 * keys_width, heads_width)
        loads += [
            load(0, q_hbm, act.at[:, q_at]),
            load(1, k_hbm, act.at[:, k_at]),
            load(2, v_hbm, act.at[:, v_at]),
            load(3, heads_hbm, act.at[:, o_at]),
        ]
        for item in loads:
            item.start()
        line.fill(1, lambda i: dot_tn(hidden[:, tile_cols(i)], dg[...]))
        line.tick(0, 1, lines)
        line.fill(2, lambda i: dot_tn(hidden[:, tile_cols(i)], du[...]))
        normed_load = load(4, normed_hbm, hidden)
        normed_load.start()
        for item in swap3.gather_late():
            swap3.gather_pass(*item)
        swap3.gather_end()
        order = swap2.order()
        for r in order[:-1]:
            swap2.scatter_start(r)
        for item in loads:
            item.wait()

        def d_head_step(rows):
            dg[rows, o_at] = dot_nt(low[rows, :], w_out[...]).astype(LOW)

        tiled(rows_all, 256, d_head_step)
        x_load = load(5, x_hbm, w_out.at[pl.ds(0, swap4.block)])
        x_load.start()
        line.tick(0, 2, lines)
        length = length_ref[0]
        score_scale = head_width ** (-0.5)
        lanes = group_size * q_block

        def stacked(ref, rows, base):
            return jnp.concatenate(
                [
                    ref[rows, pl.ds(base + i * head_width, head_width)]
                    for i in range(group_size)
                ],
                axis=0,
            )

        def pair(c):
            first = c * group_size * head_width
            for block in range(rows_all // q_block):
                rows = pl.ds(block * q_block, q_block)
                end = (block + 1) * q_block
                q2 = stacked(act, rows, first)
                do2 = stacked(dg, rows, heads_width + 2 * keys_width + first)
                keys = act[0:end, pl.ds(heads_width + c * head_width, head_width)]
                values = act[0:end, pl.ds(heads_width + keys_width + c * head_width, head_width)]
                scores = dot_nt(keys, q2) * score_scale
                k_pos = lax.broadcasted_iota(jnp.int32, (end, lanes), 0)
                q_pos = block * q_block + lax.rem(
                    lax.broadcasted_iota(jnp.int32, (1, lanes), 1), q_block
                )
                allowed = k_pos < jnp.minimum(q_pos + 1, length)
                probs = jnp.where(allowed, jnp.exp(scores - lse_ref[c, block]), 0.0)
                d_probs = dot_nt(values, do2)
                delta = jnp.sum(probs * d_probs, axis=0, keepdims=True)
                d_scores = (probs * (d_probs - delta)).astype(LOW)
                d_value = dot_nn(probs.astype(LOW), do2)
                d_key = dot_nn(d_scores, q2)
                if block:
                    dv[0 : end - q_block, :] += d_value[: end - q_block]
                    dk[0 : end - q_block, :] += d_key[: end - q_block]
                dv[end - q_block : end, :] = d_value[end - q_block :]
                dk[end - q_block : end, :] = d_key[end - q_block :]
                d_query = (dot_tn(keys, d_scores) * score_scale).T
                for i in range(group_size):
                    at = pl.ds(first + i * head_width, head_width)
                    value, gain_sum = head_back(
                        d_query[i * q_block : (i + 1) * q_block],
                        q_raw[rows, at],
                        cosine[rows, :],
                        sine[rows, :],
                        query_gain_ref[...],
                    )
                    dg[rows, at] = value.astype(LOW)
                    if c == 0 and block == 0 and i == 0:
                        query_part[...] = gain_sum
                    else:
                        query_part[...] += gain_sum
            value, gain_sum = head_back(
                dk[...] * score_scale,
                k_raw[:, pl.ds(c * head_width, head_width)],
                cosine[...],
                sine[...],
                key_gain_ref[...],
            )
            dg[:, pl.ds(heads_width + c * head_width, head_width)] = value.astype(LOW)
            if c == 0:
                key_part[...] = gain_sum
            else:
                key_part[...] += gain_sum
            dg[:, pl.ds(heads_width + keys_width + c * head_width, head_width)] = dv[...].astype(LOW)

        for c in range(pairs):
            pair(c)
            if c == 0:
                store_group(0, lines, total, turned)
        for half, r in swap2.forwards():
            swap2.scatter_forward(half, r)
        for r in order:
            rows = swap4.rows(r)

            def normed_step(cols):
                grad[rows, cols] = (
                    dot_nt(dg[rows, q_at], w_query[cols, :])
                    + dot_nt(dg[rows, k_at], w_key[cols, :])
                    + dot_nt(dg[rows, v_at], w_value[cols, :])
                ).astype(LOW)

            tiled(width, 512, normed_step)
        for sub in range(SUBS):
            local = pl.ds(sub * swap2.sub, swap2.sub)
            mixed = swap2.scatter_result(sub)
            part[swap2.rows(0, sub), :] = (
                valid_ref[local, :] * (resid_ref[local, :] + mixed)
            ).astype(LOW)
        swap2.signal(free_sem)
        pl.semaphore_wait(free_sem, swap2.bits)
        for r in order[:-1]:
            swap4.scatter_start(r)
        own2 = [
            pltpu.make_async_copy(
                part.at[swap2.rows(0, sub), :], output.at[swap2.rows(0, sub), :], own_sems.at[0, sub]
            )
            for sub in range(SUBS)
        ]
        for item in own2:
            item.start()
        normed_load.wait()
        line.tick(1, 1, lines)

        def last_tile(i):
            cols = tile_cols(i)
            return jnp.concatenate(
                [
                    dot_tn(hidden[:, cols], dg[:, pl.ds(0, heads_width + 2 * keys_width)]),
                    dot_tn(low[:, cols], act[:, o_at]),
                ],
                axis=1,
            )

        line.fill(3, last_tile)
        for half, r in swap4.forwards():
            swap4.scatter_forward(half, r)
        line.tick(1, 2, lines)
        own4 = []
        x_load.wait()
        for sub in range(SUBS):
            local = pl.ds(sub * swap4.sub, swap4.sub)
            d_normed = swap4.scatter_result(sub)
            x = w_out[local, :].astype(F32)
            c = inverse_norm(x)
            partial = jnp.sum(d_normed * (x * c), axis=0, keepdims=True)
            if sub == 0:
                in_part[...] = partial
            else:
                in_part[...] += partial
            value = d_resid[local, :] + rows_back(d_normed * in_gain_ref[...], x, c)
            grad[swap4.rows(0, sub), :] = value.astype(LOW)
            swap4.gather_start(sub)
            own4.append(
                pltpu.make_async_copy(
                    grad.at[swap4.rows(0, sub), :],
                    in_grad.at[swap4.rows(0, sub), :],
                    own_sems.at[1, sub],
                )
            )
            own4[-1].start()
        for sub in range(SUBS):
            swap2.gather_start(sub)
        store_group(1, lines, total, turned)
        for item in swap4.gather_early():
            swap4.gather_pass(*item)
        for item in swap2.gather_early():
            swap2.gather_pass(*item)
        line.tick(2, 1, lines)
        line.tick(2, 2, lines)
        store_group(2, lines, total, turned)
        for swap in (swap4, swap2):
            for item in swap.gather_late():
                swap.gather_pass(*item)
        for step in range(1, line.places - 1):
            line.tick(3, step, lines)
        store_group(3, lines, total, turned)
        for item in own2 + own4:
            item.wait()
        for swap in (swap2, swap4):
            swap.scatter_end()
            swap.gather_end()
        for group in range(line.groups):
            line.ends(group, "wait")

    def store_group(group, lines, total, turned):
        line.finish(group, lines, total)
        proj = heads_width + 2 * keys_width
        if group == 0:
            turned[...] = total[...].T
            copies = [(turned, down_out)]
        elif group == 3:
            turned[0:heads_width, :] = total[:, pl.ds(proj, heads_width)].T
            copies = [
                (total.at[:, pl.ds(0, heads_width)], query_out),
                (total.at[:, pl.ds(heads_width, keys_width)], key_out),
                (total.at[:, pl.ds(heads_width + keys_width, keys_width)], value_out),
                (turned.at[pl.ds(0, heads_width), :], proj_out),
            ]
        else:
            copies = [(total, (gate_out, up_out)[group - 1])]
        copies = [
            pltpu.make_async_copy(src, dst, final_sems.at[i])
            for i, (src, dst) in enumerate(copies)
        ]
        for copy in copies:
            copy.start()
        for copy in copies:
            copy.wait()

    pl.run_scoped(
        weights,
        pltpu.VMEM((width, units), LOW),
        pltpu.VMEM((width, units), LOW),
        pltpu.VMEM((units, width), LOW),
    )
    pl.run_scoped(
        rest,
        pltpu.VMEM((2, 2, line.tile, line.width), LOW),
        pltpu.VMEM((line.tile, line.width), F32),
        pltpu.VMEM((line.width, line.tile), F32),
        pltpu.VMEM((heads_width, width), LOW),
        pltpu.VMEM((width, heads_width), LOW),
        pltpu.VMEM((width, keys_width), LOW),
        pltpu.VMEM((width, keys_width), LOW),
        pltpu.VMEM((rows_all, heads_width), F32),
        pltpu.VMEM((rows_all, keys_width), F32),
        pltpu.VMEM((rows_all, head_width), F32),
        pltpu.VMEM((rows_all, head_width), F32),
        pltpu.VMEM((rows_all, head_width), F32),
        pltpu.VMEM((rows_all, head_width), F32),
    )


def back(
    counts, sizes, length, hidden, d_out_low, feed_weights, resid, gains, valid_rows, x_rows, lse,
    attended, tables, attn_weights,
):
    tensor_count, dp_count = counts
    rows, width = hidden.shape
    units = feed_weights[0].shape[1]
    heads_width = attn_weights[0].shape[0]
    keys_width = attn_weights[2].shape[1]
    head_width = sizes[1]
    tile = width // dp_count
    swaps = [Swap(tensor_count, rows, width) for _ in range(3)]
    line = Line(dp_count, 4, tile, units)
    vec = jax.ShapeDtypeStruct((1, width), F32)
    head_vec = jax.ShapeDtypeStruct((1, head_width), F32)
    out_shape = (
        jax.ShapeDtypeStruct((rows, width), LOW),
        jax.ShapeDtypeStruct((rows, width), LOW),
        vec,
        vec,
        head_vec,
        head_vec,
        jax.ShapeDtypeStruct((units, tile), F32),
        jax.ShapeDtypeStruct((tile, units), F32),
        jax.ShapeDtypeStruct((tile, units), F32),
        jax.ShapeDtypeStruct((tile, heads_width), F32),
        jax.ShapeDtypeStruct((tile, keys_width), F32),
        jax.ShapeDtypeStruct((tile, keys_width), F32),
        jax.ShapeDtypeStruct((heads_width, tile), F32),
        *line.outputs(),
    )
    wide = pltpu.VMEM((rows, width), LOW)
    inner = pltpu.VMEM((rows, units), LOW)
    sems = [item for swap in swaps for item in swap.semaphores()]
    return pl.pallas_call(
        functools.partial(back_kernel, (*swaps, line, sizes)),
        out_shape=out_shape,
        in_specs=[pl.BlockSpec(memory_space=pltpu.SMEM)]
        + [any_spec()] * 5
        + [vmem_spec()] * 7
        + [any_spec()] * 14,
        out_specs=(any_spec(),) * 2 + (vmem_spec(),) * 4 + (any_spec(),) * 10,
        scratch_shapes=[
            wide,
            wide,
            inner,
            inner,
            inner,
            wide,
            wide,
            pltpu.VMEM((swaps[0].block, width), F32),
            pltpu.VMEM((2, tile, units), LOW),
            pltpu.VMEM((tile, units), LOW),
            swaps[0].landing(),
            pltpu.SemaphoreType.DMA((13,)),
            pltpu.SemaphoreType.DMA((2, SUBS)),
            pltpu.SemaphoreType.DMA((4,)),
            pltpu.SemaphoreType.REGULAR,
            *sems,
            *line.semaphores(),
        ],
        compiler_params=kernel_params(1),
        name="back",
    )(
        length,
        hidden,
        d_out_low,
        *feed_weights,
        resid,
        *gains,
        valid_rows,
        lse,
        x_rows,
        *attended,
        *tables,
        *attn_weights,
    )[:13]


def rope_tables(head_width, row_count):
    half_width = head_width // 2
    inv_freq = ROPE_BASE ** (-2.0 * jnp.arange(half_width, dtype=F32) / head_width)
    angles = jnp.arange(row_count, dtype=F32)[:, None] * inv_freq[None, :]
    cosine, sine = jnp.cos(angles), jnp.sin(angles)
    return jnp.concatenate([cosine, cosine], axis=1), jnp.concatenate([-sine, sine], axis=1)


def on_device(
    tensor_count,
    dp_count,
    tokens,
    lengths,
    in_gain,
    w_query,
    w_key,
    w_value,
    query_gain,
    key_gain,
    w_out,
    post_gain,
    w_gate,
    w_up,
    w_down,
    out_grad,
):
    row_count = tokens.shape[0]
    slot_len = row_count
    head_width = query_gain.shape[0]
    q_heads = w_query.shape[1] // head_width
    kv_heads = w_key.shape[1] // head_width
    group_size = q_heads // kv_heads
    block_len = min(512, slot_len)
    block_count = slot_len // block_len
    q_block = 128
    share = row_count // tensor_count
    score_scale = head_width ** (-0.5)
    length = lengths[0]
    tensor_me = lax.axis_index("tensor")

    def own_rows(matrix):
        return lax.dynamic_slice_in_dim(matrix, tensor_me * share, share, axis=0)

    position = jnp.arange(row_count, dtype=jnp.int32)
    valid_rows = (position < length).astype(F32)[:, None]
    inputs = tokens.astype(F32)
    normed = (unit_rows(inputs) * in_gain).astype(LOW)
    q_raw = dot_nn(normed, w_query)
    k_raw = dot_nn(normed, w_key)
    values_low = dot_nn(normed, w_value).astype(LOW)
    value_heads = values_low.reshape(row_count, kv_heads, head_width)
    tables = rope_tables(head_width, slot_len)

    def prepare(raw, heads, gain):
        normed_heads = norm_rows(raw.reshape(row_count, heads, head_width), gain)
        half = head_width // 2
        other = jnp.concatenate([normed_heads[..., half:], normed_heads[..., :half]], axis=-1)
        turned = normed_heads * tables[0][:, None] + other * tables[1][:, None]
        return turned.astype(LOW)

    query_low = prepare(q_raw, q_heads, query_gain)
    keys_low = prepare(k_raw, kv_heads, key_gain)
    query_groups = query_low.reshape(row_count, kv_heads, group_size, head_width)
    log_totals = []
    heads = []
    for block in range(block_count):
        rows = slice(block * block_len, (block + 1) * block_len)
        key_end = (block + 1) * block_len
        scores = masked_scores(
            query_groups[rows], keys_low[:key_end], length, block * block_len, score_scale
        )
        row_peak = jnp.max(scores, axis=-1, keepdims=True)
        exponent = jnp.exp(scores - row_peak)
        row_total = jnp.sum(exponent, axis=-1, keepdims=True)
        probs_low = (exponent / row_total).astype(LOW)
        head_blk = (
            jnp.einsum("cgqk,kcd->qcgd", probs_low, value_heads[:key_end], preferred_element_type=F32)
            .reshape(block_len, q_heads * head_width)
            .astype(LOW)
        )
        log_totals.append((row_peak + jnp.log(row_total))[..., 0])
        heads.append(head_blk)
    heads_low = jnp.concatenate(heads, axis=0)
    lse = (
        jnp.concatenate(log_totals, axis=2)
        .reshape(kv_heads, group_size, row_count // q_block, q_block)
        .transpose(0, 2, 1, 3)
        .reshape(kv_heads, row_count // q_block, 1, group_size * q_block)
    )
    resid, hidden = out_sum(tensor_count, heads_low, w_out, own_rows(tokens), post_gain)
    d_out_low = (out_grad.astype(F32) * valid_rows).astype(LOW)
    (
        output,
        in_grad,
        post_part,
        in_part,
        query_part,
        key_part,
        grad_down,
        grad_gate,
        grad_up,
        grad_query,
        grad_key,
        grad_value,
        grad_out,
    ) = back(
        (tensor_count, dp_count),
        (q_block, head_width, kv_heads, group_size),
        lengths,
        hidden,
        d_out_low,
        (w_gate, w_up, w_down),
        resid,
        (post_gain[None], in_gain[None], query_gain[None], key_gain[None]),
        own_rows(valid_rows),
        own_rows(tokens),
        lse,
        (
            query_low.reshape(row_count, -1),
            keys_low.reshape(row_count, -1),
            values_low,
            heads_low,
            normed,
            q_raw,
            k_raw,
        ),
        tables,
        (w_out, w_query, w_key, w_value),
    )
    grad_in_gain, grad_query_gain, grad_key_gain, grad_post_gain = lax.psum(
        (in_part[0], query_part[0], key_part[0], post_part[0]), ("dp", "tensor")
    )
    return (
        output,
        in_grad,
        grad_in_gain,
        grad_query,
        grad_key,
        grad_value,
        grad_query_gain,
        grad_key_gain,
        grad_out,
        grad_post_gain,
        grad_gate,
        grad_up,
        grad_down,
    )


def solution(mesh):
    tensor_count, dp_count = mesh.shape["tensor"], mesh.shape["dp"]

    def layer(*args):
        return on_device(tensor_count, dp_count, *args)

    return jax.shard_map(
        layer,
        mesh=mesh,
        in_specs=(
            P("dp", None),
            P("dp"),
            P(),
            P(None, "tensor"),
            P(None, "tensor"),
            P(None, "tensor"),
            P(),
            P(),
            P("tensor", None),
            P(),
            P(None, "tensor"),
            P(None, "tensor"),
            P("tensor", None),
            P("dp", None),
        ),
        out_specs=(
            P("dp", None),
            P("dp", None),
            P(),
            P("dp", "tensor"),
            P("dp", "tensor"),
            P("dp", "tensor"),
            P(),
            P(),
            P("tensor", "dp"),
            P(),
            P("dp", "tensor"),
            P("dp", "tensor"),
            P("tensor", "dp"),
        ),
        check_vma=False,
    )
```

time: 675 us -> 549 us (0.81)
  waiting for transfers between devices: 260 us -> 0 us
  Pallas kernels: 189 us -> 407 us
  matrix products: 74.8 us -> 15.4 us
  other arithmetic: 57.4 us -> 32.2 us
  local copies, waits for them, and re-layouts: 23.8 us -> 46.1 us
  between operations: 17.2 us -> 1.97 us
    pallas_call x1, Pallas kernels: 109 us -> 327 us  [back(): pl.pallas_call(functools.partial(back_kernel, (*swaps, line, sizes)), out...]
    psum x1 -> x0, waiting for transfers between devices: 145 us -> none  [on_device(): mixed = lax.psum(dot_nn(act, w_down).astype(LOW), 'tensor')]
    reduce_scatter x7 -> x0, waiting for transfers between devices: 111 us -> none  [over_dp(): lax.psum_scatter(grad, 'dp', scatter_dimension=0, tiled=True).astype(F32)]
    dot_general x18 -> x2, matrix products: 52.2 us -> 4.17 us  [on_device(): jnp.einsum('cgqk,kcd->qcgd', probs_low, value_heads[:key_end], preferred_...]
    convert_element_type x13 -> x3, other arithmetic: 29 us -> 8.12 us  [prepare(): return turned.astype(LOW)]
    mul x0 -> x9, local copies, waits for them, and re-layouts: none -> 15.9 us  [the longest x4 7.62 us: prepare(): turned = normed_heads * tables[0][:, None] + other * tables[1][:, None]]
    dot_general x4 -> x3, matrix products: 18.2 us -> 8.81 us  [dot_nn(): return jnp.dot(left, right, preferred_element_type=F32)]
    unnamed x93 -> x74, local copies, waits for them, and re-layouts: 15.7 us -> 17 us
  transfers between devices with their start and end apart: 10 -> 0, of which waited for: 4 -> 0; matrix products, arithmetic and copies ran while one was open for 8% -> 0% of each run, Pallas kernels for 0% -> 0%
where the time goes in v2:
time: 549 us; the launch traced here: 543 us
  Pallas kernels  407 us (74%)
  local copies, waits for them, and re-layouts  46.1 us (8%)
  blocking collectives  40.3 us (7%)
  other arithmetic  32.2 us (6%)
  matrix products  15.4 us (3%)
    pallas_call x1, Pallas kernels, back(): pl.pallas_call(functools.partial(back_kernel, (*swaps, line, sizes)), out...  327 us
    pallas_call x1, Pallas kernels, out_sum(): pl.pallas_call(functools.partial(out_kernel, swap), out_shape=(jax.ShapeD...  79.7 us
    psum x1, blocking collectives, on_device(): lax.psum((in_part[0], query_part[0], key_part[0], post_part[0]), ('dp', '...  40.3 us
    unnamed x74, local copies, waits for them, and re-layouts  17 us

profile of v2, /device:TPU:0, one launch (start us, length us, event | category | flops | bytes accessed | tf_op | source)
XLA Modules:
  0.0 543.0 jit_solution(15008284185717198740)
XLA Ops:
  1.3 0.7 broadcast_bitcast_fusion.1
  2.0 0.7 broadcast_bitcast_fusion
  2.6 3.1 fusion
  5.8 0.8 copy.84.refs_11_
  6.6 0.1 fusion.15
  6.8 1.2 fusion.8
  7.9 2.3 constant_dynamic-slice_fusion.x_ref.refs_13_
  10.3 2.0 fusion.21
  12.2 0.3 pad_maximum_fusion.1
  12.6 1.2 copy.66
  13.8 1.0 copy.67
  14.8 1.3 mul.213.clone
  16.1 1.3 mul.222
  17.4 2.1 copy.99
  19.5 3.3 fusion.2.refs_18_
  22.8 2.0 copy-done.2
  24.8 1.2 convolution_convert_fusion.refs_16_
  26.1 0.9 copy.94
  27.0 1.0 copy.96
  28.0 3.8 multiply_reduce_fusion.1
  31.9 0.2 copy.101
  32.1 2.0 mul.206.clone
  34.1 0.3 copy.65
  34.5 1.6 copy.81.refs_20_
  36.1 0.3 multiply_multiply_fusion.1
  36.4 0.3 fusion.30
  36.8 1.4 fusion.22
  38.2 1.1 fusion.13.refs_15_
  39.4 0.2 copy-done.3
  39.5 0.8 copy-done.13
  40.3 3.8 multiply_reduce_fusion
  44.1 1.9 copy.77.refs_19_
  46.1 2.8 multiply_multiply_fusion
  48.9 0.2 fusion.28
  49.1 0.2 copy-done.15
  49.3 2.1 add_convert_fusion.1
  51.4 2.9 copy.100
  54.2 1.1 fusion.29
  55.3 1.6 mul.218
  56.9 3.4 copy.98
  60.3 4.9 add_convert_fusion.refs_14_
  65.3 0.9 fusion.7
  66.1 0.9 fusion.6
  67.1 1.5 fusion.11
  68.6 0.2 copy.95
  68.8 5.0 multiply_convert_fusion.refs_2_
  73.9 1.6 fusion.4
  75.5 1.9 fusion.3
  77.3 2.7 fusion.10
  80.0 0.6 pad_maximum_fusion.3
  80.7 0.2 copy.97
  80.9 1.0 pad_maximum_fusion.heads_ref.refs_17_
  81.9 79.7 %out_sum.1 = (f32[256,2048]{1,0:T(8,128)}, bf16[1024,2048]{1,0:T(8,128)(2,1)}) custom-call(bf16[1024,512]{1,0:T(8,128)(2,1)} %pad_maximum_fusion.heads_ref.refs_17_, bf16[512,2048]{1,0:T(8,128)(2,1)} %refs_23_.1, bf16[256,2048]{1,0:T(8,128)(2,1)} %constant_dynamic-slice_fusion.x_ref.refs_13_, f32[1,2048]{1,0:T(1,128)} %bitcast.131), custom_call_target="tpu_custom_call" | custom-call | tf_op jit(solution)/shard_map/out_sum/pallas_call | solution.py:309
  161.6 327.3 %back.1 = (bf16[1024,2048]{1,0:T(8,128)(2,1)}, bf16[1024,2048]{1,0:T(8,128)(2,1)}, f32[1,2048]{1,0:T(1,128)}, f32[1,2048]{1,0:T(1,128)}, f32[1,128]{1,0:T(1,128)...) custom-call(s32[1]{0:T(128)} %copy.119.refs_0_, ...), custom_call_target="tpu_custom_call" | custom-call | tf_op jit(solution)/shard_map/back/pallas_call | solution.py:1010
  489.0 40.3 %all-reduce = (f32[2048]{0:T(1024)}, f32[128]{0:T(128)}, f32[128]{0:T(128)}, f32[2048]{0:T(1024)}) all-reduce(f32[2048]{0:T(1024)} %bitcast.135, f32[128]{0:T(128)} %bitcast.138, f32[128]{0:T(128)} %bitcast.139, f32[2048]{0:T(1024)} %bitcast.134), channel_id=1, replica_groups=mesh['dp'=8,'tensor'=4] {'dp','tensor'}, use_global_device_ids=true, to_apply=%region_7.8 | all-reduce | flops 4352 | bytes 34816 | tf_op jit(solution)/shard_map/psum | solution.py:1184
  529.3 4.9 copy.120
  534.3 2.1 copy.121
  536.4 0.8 copy.122
  537.2 0.7 copy.123
  537.9 0.7 copy.124
  538.6 0.8 copy.125
  539.4 1.1 copy.126
  540.6 1.1 copy.127
  541.7 1.1 copy.128
  (71 shorter events, 0.3 us)
Async XLA Ops:
  12.6 24.2 %copy-start.4 = (f32[1024,128]{1,0:T(8,128)}, f32[1024,128]{1,0:T(8,128)S(1)}, u32[]{:S(2)}) copy-start(f32[1024,128]{1,0:T(8,128)S(1)} %get-tuple-element.70.refs_21_) | copy-start | bytes 1572868
  12.6 24.2 %copy-start.6 = (f32[1024,128]{1,0:T(8,128)}, f32[1024,128]{1,0:T(8,128)S(1)}, u32[]{:S(2)}) copy-start(f32[1024,128]{1,0:T(8,128)S(1)} %get-tuple-element.71.refs_22_) | copy-start | bytes 1572868
  14.8 4.8 copy-start.29
  19.5 5.3 copy-start.19
  22.8 2.0 copy-start.2
  26.1 1.9 copy-start.12
  31.8 2.3 copy-start.11
  31.9 4.2 copy-start.31
  36.0 2.2 copy-start.5
  36.4 1.8 copy-start.8
  36.4 1.8 copy-start.9
  36.8 2.8 copy-start.3
  36.8 3.5 copy-start.13
  44.1 2.0 copy-start.30
  46.1 14.2 %copy-start = (f32[1024,512]{1,0:T(8,128)}, f32[1024,512]{1,0:T(8,128)S(1)}, u32[]{:S(2)}) copy-start(f32[1024,512]{1,0:T(8,128)S(1)} %copy.77.refs_19_) | copy-start | bytes 6291460
  46.1 3.0 copy-start.1
  46.1 3.1 copy-start.7
  46.1 3.2 copy-start.15
  60.3 5.0 copy-start.20
  60.3 5.0 copy-start.25
  65.3 1.8 copy-start.26
  68.8 5.1 copy-start.14
  68.8 5.0 copy-start.24
  75.4 1.9 copy-start.21
  529.3 4.9 copy-start.10
  534.2 2.2 copy-start.23
  534.2 3.0 copy-start.28
  534.2 3.7 copy-start.27
  534.2 4.4 copy-start.22
  534.2 5.2 copy-start.18
  536.4 4.2 copy-start.17
  537.2 4.5 copy-start.16

commit v3 on v2

v3 whole, which is shorter than its diff:
```python
import functools

import jax
import jax.numpy as jnp
import numpy as np
from jax import lax
from jax.experimental import pallas as pl
from jax.experimental.pallas import tpu as pltpu
from jax.sharding import PartitionSpec as P

NORM_EPS = 1e-06
ROPE_BASE = 1000000.0
MASK_FILL = -1e30
LOW = jnp.bfloat16
F32 = jnp.float32
MESH = pl.DeviceIdType.MESH
VMEM_BYTES = 63 * 1024 * 1024
CHUNK = 256
KEYS = 256


def unit_rows(matrix):
    return matrix * lax.rsqrt(jnp.mean(matrix * matrix, axis=-1, keepdims=True) + NORM_EPS)


def dot_nn(left, right):
    return jnp.dot(left, right, preferred_element_type=F32)


def dot_tn(left, right):
    return lax.dot_general(left, right, (((0,), (0,)), ((), ())), preferred_element_type=F32)


def dot_nt(left, right):
    return lax.dot_general(left, right, (((1,), (1,)), ((), ())), preferred_element_type=F32)


class Swap:
    def __init__(self, count, rows, width):
        self.count, self.width = count, width
        self.bits = count.bit_length() - 1
        self.chunk = min(CHUNK, rows)
        self.chunks = rows // self.chunk
        self.block = self.chunk // count
        self.half = width // 2
        self.orders = [list(range(self.bits)), list(range(self.bits))[::-1]]
        self.slots = []
        for order in self.orders:
            slot = {}
            for step in range(self.bits):
                for r in range(count):
                    if not any(r >> b & 1 for b in order[: step + 1]):
                        slot[step, r] = len(slot)
            self.slots.append(slot)

    def landing(self):
        return pltpu.VMEM((2, self.count - 1, self.chunks * self.block, self.half), LOW)

    def semaphores(self):
        n, c = self.count, self.chunks
        return [
            pltpu.SemaphoreType.DMA((2, n, c)),
            pltpu.SemaphoreType.DMA((2, n, c)),
            pltpu.SemaphoreType.DMA((2, n * self.bits, c)),
            pltpu.SemaphoreType.DMA((2, n, c)),
        ]

    def bind(self, part, recv, dest, sems, own=None):
        self.part, self.recv, self.dest, self.sems = part, recv, dest, sems
        self.own = dest if own is None else own
        self.me = lax.axis_index("tensor")
        return self

    def near(self, bit):
        own = (self.me // 2**bit) % 2
        return self.me + (1 - 2 * own) * 2**bit

    def rows(self, r, c):
        owner = self.me
        for bit in range(self.bits):
            if r >> bit & 1:
                owner = owner + (1 - 2 * ((self.me // 2**bit) % 2)) * 2**bit
        return pl.ds(pl.multiple_of(c * self.chunk + owner * self.block, self.block), self.block)

    def local(self, c):
        return pl.ds(c * self.block, self.block)

    def columns(self, half):
        return pl.ds(half * self.half, self.half)

    def signal(self, sem):
        for bit in range(self.bits):
            pl.semaphore_signal(
                sem, inc=1, device_id={"tensor": self.near(bit)}, device_id_type=MESH
            )

    def order(self):
        return sorted(range(1, self.count), key=lambda r: (-bin(r).count("1"), r))

    def first(self, half, r):
        return next(k for k, bit in enumerate(self.orders[half]) if r >> bit & 1)

    def scatter_copy(self, half, r, c):
        step = self.first(half, r)
        bit = self.orders[half][step]
        slot = self.slots[half][step, r ^ (1 << bit)]
        return pltpu.make_async_remote_copy(
            src_ref=self.part.at[self.rows(r, c), self.columns(half)],
            dst_ref=self.recv.at[half, slot, self.local(c)],
            send_sem=self.sems[0].at[half, r, c],
            recv_sem=self.sems[1].at[half, slot, c],
            device_id={"tensor": self.near(bit)},
            device_id_type=MESH,
        )

    def scatter_wait(self, half, step, r, c):
        slot = self.slots[half][step, r]
        ref = self.recv.at[half, slot, self.local(c)]
        pltpu.make_async_copy(ref, ref, self.sems[1].at[half, slot, c]).wait()
        return ref

    def scatter_start(self, c):
        for r in self.order():
            for half in range(2):
                if self.first(half, r) == 0:
                    self.scatter_copy(half, r, c).start()

    def scatter_forward(self, c):
        todo = [
            (self.first(half, r), half, r)
            for half in range(2)
            for r in range(1, self.count)
            if self.first(half, r) > 0
        ]
        for step, half, r in sorted(todo):
            where = self.rows(r, c), self.columns(half)
            total = self.part[where].astype(F32)
            for j in range(step):
                total = total + self.scatter_wait(half, j, r, c)[...].astype(F32)
            self.part[where] = total.astype(LOW)
            self.scatter_copy(half, r, c).start()

    def scatter_result(self, c):
        total = []
        for half in range(2):
            value = self.part[self.rows(0, c), self.columns(half)].astype(F32)
            for j in range(self.bits):
                value = value + self.scatter_wait(half, j, 0, c)[...].astype(F32)
            total.append(value)
        return jnp.concatenate(total, axis=1)

    def scatter_end(self, c):
        for half in range(2):
            for r in range(1, self.count):
                self.scatter_copy(half, r, c).wait_send()

    def last(self, half, r):
        order = self.orders[half][::-1]
        return max([-1] + [j for j, bit in enumerate(order) if r >> bit & 1])

    def gather_copy(self, half, r, step, c):
        bit = self.orders[half][::-1][step]
        where = self.rows(r, c), self.columns(half)
        return pltpu.make_async_remote_copy(
            src_ref=self.dest.at[where] if r else self.own.at[where],
            dst_ref=self.dest.at[where],
            send_sem=self.sems[2].at[half, r * self.bits + step, c],
            recv_sem=self.sems[3].at[half, r ^ (1 << bit), c],
            device_id={"tensor": self.near(bit)},
            device_id_type=MESH,
        )

    def gather_start(self, c):
        for step in range(self.bits):
            for half in range(2):
                self.gather_copy(half, 0, step, c).start()

    def gather_pass(self, c, late):
        todo = [
            (self.last(half, r), bin(r).count("1"), half, r)
            for half in range(2)
            for r in range(1, self.count)
        ]
        for step, _, half, r in sorted(todo):
            if (step == self.bits - 1) != late:
                continue
            ref = self.dest.at[self.rows(r, c), self.columns(half)]
            pltpu.make_async_copy(ref, ref, self.sems[3].at[half, r, c]).wait()
            for later in range(step + 1, self.bits):
                self.gather_copy(half, r, later, c).start()

    def gather_end(self, c):
        for half in range(2):
            for r in range(self.count):
                for step in range(self.last(half, r) + 1, self.bits):
                    self.gather_copy(half, r, step, c).wait_send()


class Line:
    def __init__(self, count, groups, tile, width):
        self.count, self.groups, self.tile, self.width = count, groups, tile, width
        self.places = count // 2

    def outputs(self):
        shape = (self.tile, self.width)
        return [
            jax.ShapeDtypeStruct((self.groups, self.places) + shape, LOW),
            jax.ShapeDtypeStruct((self.groups, self.places) + shape, LOW),
            jax.ShapeDtypeStruct((self.groups, self.places + 1) + shape, LOW),
        ]

    def semaphores(self):
        g, n = self.groups, self.places
        return [
            pltpu.SemaphoreType.DMA((g, n)),
            pltpu.SemaphoreType.DMA((g, n)),
            pltpu.SemaphoreType.DMA((2,)),
            pltpu.SemaphoreType.DMA((2, g, n)),
            pltpu.SemaphoreType.DMA((g, n + 1)),
            pltpu.SemaphoreType.DMA((6,)),
        ]

    def bind(self, core_land, acc, land, stage, extra, sems):
        self.core_land, self.acc, self.land = core_land, acc, land
        self.stage, self.extra = stage, extra
        (
            self.core_send,
            self.core_recv,
            self.stage_sem,
            self.line_send,
            self.line_recv,
            self.local_sem,
        ) = sems
        self.me = lax.axis_index("dp")
        self.place = self.me // 2
        self.core = self.me % 2
        self.other = self.me + 1 - 2 * self.core
        self.before = []
        return self

    def signal(self, sem):
        @pl.when(self.place > 0)
        def _():
            pl.semaphore_signal(sem, inc=1, device_id={"dp": self.me - 2}, device_id_type=MESH)

        @pl.when(self.place < self.places - 1)
        def _():
            pl.semaphore_signal(sem, inc=1, device_id={"dp": self.me + 2}, device_id_type=MESH)

    def peers(self):
        ends = (self.places - 1 - self.place) // (self.places - 1) + self.place // (self.places - 1)
        return 2 - ends

    def core_copy(self, group, i, slot):
        return pltpu.make_async_remote_copy(
            src_ref=self.stage.at[slot],
            dst_ref=self.core_land.at[group, i],
            send_sem=self.core_send.at[group, i],
            recv_sem=self.core_recv.at[group, i],
            device_id={"dp": self.other},
            device_id_type=MESH,
        )

    def fill(self, group, tile_of):
        def away(i, carry):
            slot = lax.rem(i, 2)

            @pl.when(i >= 2)
            def _():
                self.core_copy(group, i - 2, slot).wait_send()

            for cols, value in tile_of(2 * i + 1 - self.core):
                self.stage[slot, :, cols] = value.astype(LOW)
            self.core_copy(group, i, slot).start()
            return carry

        lax.fori_loop(0, self.places, away, 0)
        for i in range(max(0, self.places - 2), self.places):
            self.core_copy(group, i, i % 2).wait_send()

        def store(i, slot):
            return pltpu.make_async_copy(
                self.stage.at[slot], self.acc.at[group, i], self.stage_sem.at[slot]
            )

        def home(i, carry):
            slot = lax.rem(i, 2)
            landed = self.core_land.at[group, i]
            pltpu.make_async_copy(landed, landed, self.core_recv.at[group, i]).wait()
            fetch = pltpu.make_async_copy(landed, self.extra, self.local_sem.at[0])
            fetch.start()

            @pl.when(i >= 2)
            def _():
                store(i - 2, slot).wait()

            for spot, (cols, value) in enumerate(tile_of(2 * i + self.core)):
                if spot == 0:
                    fetch.wait()
                self.stage[slot, :, cols] = (value + self.extra[:, cols].astype(F32)).astype(LOW)
            store(i, slot).start()
            return carry

        lax.fori_loop(0, self.places, home, 0)
        for i in range(max(0, self.places - 2), self.places):
            store(i, i % 2).wait()
        self.ends(group, "start")

    def line_copy(self, group, way, j, source):
        if way == 0:
            slot, to = j, self.me + 2
        else:
            final = 1 - jnp.minimum(self.place - 1 - j, 1)
            slot, to = j + final * (self.places - j), self.me - 2
        return pltpu.make_async_remote_copy(
            src_ref=source,
            dst_ref=self.land.at[group, slot],
            send_sem=self.line_send.at[way, group, j],
            recv_sem=self.line_recv.at[group, slot],
            device_id={"dp": to},
            device_id_type=MESH,
        )

    def ends(self, group, act):
        n = self.places

        @pl.when(self.place == 0)
        def _():
            for j in range(n - 1, 0, -1):
                copy = self.line_copy(group, 0, j, self.acc.at[group, j])
                copy.start() if act == "start" else copy.wait_send()

        @pl.when(self.place == n - 1)
        def _():
            for j in range(n - 1):
                copy = self.line_copy(group, 1, j, self.acc.at[group, j])
                copy.start() if act == "start" else copy.wait_send()

    def landed(self, group, slot):
        ref = self.land.at[group, slot]
        pltpu.make_async_copy(ref, ref, self.line_recv.at[group, slot]).wait()
        return ref

    def on_way(self, step, way):
        far = self.place if way == 0 else self.places - 1 - self.place
        index = self.places - 1 - step + self.place if way == 0 else step - far
        return jnp.logical_and(far >= 1, far <= step), index

    def settle(self, lines):
        for group, step in self.before:
            for way in range(2):
                active, j = self.on_way(step, way)

                @pl.when(active)
                def _(way=way, j=j, group=group):
                    self.line_copy(group, way, j, lines.at[way, 0]).wait_send()

        self.before = []

    def tick(self, group, step, lines):
        self.settle(lines)
        for way in range(2):
            active, j = self.on_way(step, way)

            @pl.when(active)
            def _(way=way, j=j):
                here = pltpu.make_async_copy(
                    self.acc.at[group, j], lines.at[way, 0], self.local_sem.at[2 * way]
                )
                here.start()
                there = pltpu.make_async_copy(
                    self.landed(group, j), lines.at[way, 1], self.local_sem.at[2 * way + 1]
                )
                there.start()
                here.wait()
                there.wait()
                lines[way, 0] = (
                    lines[way, 0].astype(F32) + lines[way, 1].astype(F32)
                ).astype(LOW)
                self.line_copy(group, way, j, lines.at[way, 0]).start()

        self.before = [(group, step)]

    def finish(self, group, lines, total):
        self.settle(lines)
        n = self.places
        here = pltpu.make_async_copy(
            self.acc.at[group, self.place], lines.at[0, 0], self.local_sem.at[0]
        )
        here.start()
        here.wait()
        total[...] = lines[0, 0].astype(F32)

        @pl.when(self.place > 0)
        def _():
            there = pltpu.make_async_copy(
                self.landed(group, self.place), lines.at[0, 1], self.local_sem.at[1]
            )
            there.start()
            there.wait()
            total[...] += lines[0, 1].astype(F32)

        @pl.when(self.place < n - 1)
        def _():
            there = pltpu.make_async_copy(
                self.landed(group, n), lines.at[1, 1], self.local_sem.at[2]
            )
            there.start()
            there.wait()
            total[...] += lines[1, 1].astype(F32)


class Spread:
    def __init__(self, counts, length):
        tensor_count, dp_count = counts
        self.length = length
        self.steps = [("tensor", 2**b) for b in range(tensor_count.bit_length() - 1)]
        self.steps += [("dp", 2**b) for b in range(dp_count.bit_length() - 1)]

    def scratch(self):
        n = len(self.steps)
        return [
            pltpu.VMEM((n + 1, 1, self.length), F32),
            pltpu.VMEM((n, 1, self.length), F32),
            pltpu.SemaphoreType.DMA((n,)),
            pltpu.SemaphoreType.DMA((n,)),
        ]

    def bind(self, mine, land, send, recv):
        self.mine, self.land, self.send, self.recv = mine, land, send, recv
        return self

    def partner(self, step):
        axis, size = self.steps[step]
        me = lax.axis_index(axis)
        return {axis: me + (1 - 2 * ((me // size) % 2)) * size}

    def signal(self, sem):
        for step in range(len(self.steps)):
            pl.semaphore_signal(
                sem, inc=1, device_id=self.partner(step), device_id_type=MESH
            )

    def copy(self, step):
        return pltpu.make_async_remote_copy(
            src_ref=self.mine.at[step],
            dst_ref=self.land.at[step],
            send_sem=self.send.at[step],
            recv_sem=self.recv.at[step],
            device_id=self.partner(step),
            device_id_type=MESH,
        )

    def next(self, step):
        self.copy(step).wait()
        self.mine[step + 1] = self.mine[step] + self.land[step]
        if step + 1 < len(self.steps):
            self.copy(step + 1).start()


def tiled(total, size, body):
    count = total // size

    def step(i, carry):
        body(pl.ds(pl.multiple_of(i * size, size), size))
        return carry

    lax.fori_loop(0, count, step, 0)


def any_spec():
    return pl.BlockSpec(memory_space=pl.ANY)


def vmem_spec():
    return pl.BlockSpec(memory_space=pltpu.VMEM)


def kernel_params(identity):
    return pltpu.CompilerParams(
        collective_id=identity, has_side_effects=True, vmem_limit_bytes=VMEM_BYTES
    )


def head_forward(raw, cosine, sine, gain):
    width = raw.shape[-1]
    unit = raw * lax.rsqrt(jnp.mean(raw * raw, axis=-1, keepdims=True) + NORM_EPS) * gain
    return (unit * cosine + pltpu.roll(unit, width // 2, 1) * sine).astype(LOW)


def head_back(grad, raw, cosine, sine, gain):
    width = raw.shape[-1]
    turned = grad * cosine - pltpu.roll(grad, width // 2, 1) * sine
    scale = lax.rsqrt(jnp.mean(raw * raw, axis=-1, keepdims=True) + NORM_EPS)
    unit = raw * scale
    gain_sum = jnp.sum(turned * unit, axis=0, keepdims=True)
    inner = turned * gain
    return scale * (inner - unit * jnp.mean(inner * unit, axis=-1, keepdims=True)), gain_sum


def rows_back(d_unit, rows, scale):
    unit = rows * scale
    return scale * (d_unit - unit * jnp.mean(d_unit * unit, axis=-1, keepdims=True))


def inverse_norm(rows):
    return lax.rsqrt(jnp.mean(rows * rows, axis=-1, keepdims=True) + NORM_EPS)


def layer_kernel(plan, *refs):
    swap1, swap3, swap2, swap4, line, spread, sizes = plan
    q_block, head_width, pairs, group_size = sizes
    refs = iter(refs)

    def take(count):
        return [next(refs) for _ in range(count)]

    length_ref, in_gain_ref, post_gain_ref, query_gain_ref, key_gain_ref = take(5)
    tokens_hbm, grad_hbm, cos_hbm, sin_hbm = take(4)
    w_query_hbm, w_key_hbm, w_value_hbm, w_out_hbm = take(4)
    wg_hbm, wu_hbm, wd_hbm = take(3)
    output, in_grad, gains_out = take(3)
    down_out, gate_out, up_out, query_out, key_out, value_out, proj_out = take(7)
    core_land, acc, land, normed_hbm, heads_hbm, q_raw_hbm, k_raw_hbm, resid_hbm = take(8)
    hidden, grad, act, dg, du, part, low, resid, stage, extra, flip, recv = take(12)
    w_query, w_key, w_value, w_out, cosine, sine, lse = take(7)
    in_sems, token_sems, front_sems, own_sems, final_sems, free_sem = take(6)
    swap1.bind(part, recv, hidden, take(4))
    swap3.bind(part, recv, low, take(4))
    swap2.bind(part, recv, output, take(4), own=part)
    swap4.bind(grad, recv, in_grad, take(4), own=grad)
    line.bind(core_land, acc, land, stage, extra, take(6))
    spread.bind(*take(4))

    rows_all, units = act.shape
    width = swap1.width
    heads_width, keys_width = w_query.shape[1], w_key.shape[1]
    unit_tile = 256
    chunk, chunks = swap1.chunk, swap1.chunks
    score_scale = head_width ** (-0.5)
    lanes = group_size * q_block
    length = length_ref[0]
    post_part = spread.mine.at[0, :, pl.ds(0, width)]
    in_part = spread.mine.at[0, :, pl.ds(width, width)]
    query_part = spread.mine.at[0, :, pl.ds(2 * width, head_width)]
    key_part = spread.mine.at[0, :, pl.ds(2 * width + head_width, head_width)]
    q_at = pl.ds(0, heads_width)
    k_at = pl.ds(heads_width, keys_width)
    v_at = pl.ds(heads_width + keys_width, keys_width)
    o_at = pl.ds(heads_width + 2 * keys_width, heads_width)

    def head_at(base, i):
        return pl.ds(base.start + i * head_width, head_width)

    def load(i, src, dst):
        return pltpu.make_async_copy(src, dst, in_sems.at[i])

    def chunk_rows(c):
        return pl.ds(c * chunk, chunk)

    def valid(rows):
        return rows.start + lax.broadcasted_iota(jnp.int32, (rows.size, 1), 0) < length

    def stacked(ref, rows, base, c):
        return jnp.concatenate(
            [ref[rows, head_at(base, c * group_size + i)] for i in range(group_size)], axis=0
        )

    def allowed_of(block, start, stop):
        k_pos = start + lax.broadcasted_iota(jnp.int32, (stop - start, lanes), 0)
        q_pos = block * q_block + lax.rem(
            lax.broadcasted_iota(jnp.int32, (1, lanes), 1), q_block
        )
        return k_pos < jnp.minimum(q_pos + 1, length)

    def tile_cols(i):
        return pl.ds(pl.multiple_of(i * line.tile, line.tile), line.tile)

    def products(left, right, cuts):
        def tile_of(i):
            flip[...] = left[:, tile_cols(i)].T
            for start in range(*cuts):
                cols = pl.ds(start, cuts[2])
                yield cols, dot_nn(flip[...], right[:, cols])

        return tile_of

    def add_to(ref, value, first):
        if first:
            ref[...] = value
        else:
            ref[...] += value


    def front(wd, wg, wu, q_raw, k_raw):
        attn_loads = [
            load(0, w_query_hbm, w_query),
            load(1, w_key_hbm, w_key),
            load(2, w_value_hbm, w_value),
            load(3, cos_hbm, cosine),
            load(4, sin_hbm, sine),
            load(5, w_out_hbm, w_out),
        ]
        feed_loads = [
            load(6, wg_hbm, wg),
            load(7, wu_hbm, wu),
            load(8, grad_hbm, grad),
            load(9, wd_hbm, wd),
        ]
        token_loads = [
            pltpu.make_async_copy(
                tokens_hbm.at[chunk_rows(c)], low.at[chunk_rows(c)], token_sems.at[c]
            )
            for c in range(chunks)
        ]
        for item in token_loads[:1] + attn_loads + token_loads[1:] + feed_loads:
            item.start()
        barrier = pltpu.get_barrier_semaphore()
        spread.signal(barrier)
        line.signal(barrier)
        pl.semaphore_wait(barrier, len(spread.steps) + line.peers())

        def front_store(i, src, dst):
            return pltpu.make_async_copy(src, dst, front_sems.at[i])

        raw_stores = []

        def attend(c):
            rows = chunk_rows(c)
            token_loads[c].wait()

            def norm_step(local):
                at = pl.ds(c * chunk + local.start, local.size)
                x = low[at, :].astype(F32)
                hidden[at, :] = (unit_rows(x) * in_gain_ref[...]).astype(LOW)

            tiled(chunk, 32, norm_step)
            store = front_store(0, hidden.at[rows], normed_hbm.at[rows])
            store.start()
            if c == 0:
                for item in attn_loads:
                    item.wait()
            for item in raw_stores:
                item.wait()
            raw_stores.clear()
            q_raw[...] = dot_nn(hidden[rows, :], w_query[...])
            k_raw[...] = dot_nn(hidden[rows, :], w_key[...])
            du[rows, v_at] = dot_nn(hidden[rows, :], w_value[...]).astype(LOW)
            for raw, base, gain in ((q_raw, q_at, query_gain_ref), (k_raw, k_at, key_gain_ref)):
                for i in range(base.size // head_width):
                    du[rows, head_at(base, i)] = head_forward(
                        raw[:, pl.ds(i * head_width, head_width)],
                        cosine[rows, :],
                        sine[rows, :],
                        gain[...],
                    )
            raw_stores.append(front_store(1, q_raw, q_raw_hbm.at[rows]))
            raw_stores.append(front_store(2, k_raw, k_raw_hbm.at[rows]))
            for item in raw_stores:
                item.start()
            for pair in range(pairs):
                for piece in range(chunk // q_block):
                    block = c * (chunk // q_block) + piece
                    q_rows = pl.ds(block * q_block, q_block)
                    end = (block + 1) * q_block
                    queries = stacked(du, q_rows, q_at, pair)
                    peak = total = sums = None
                    for start in range(0, end, KEYS):
                        stop = min(start + KEYS, end)
                        scores = dot_nt(du[start:stop, head_at(k_at, pair)], queries) * score_scale
                        scores = jnp.where(allowed_of(block, start, stop), scores, MASK_FILL)
                        top = jnp.max(scores, axis=0, keepdims=True)
                        new_peak = top if peak is None else jnp.maximum(peak, top)
                        exponent = jnp.exp(scores - new_peak)
                        add = jnp.sum(exponent, axis=0, keepdims=True)
                        more = dot_tn(du[start:stop, head_at(v_at, pair)], exponent.astype(LOW))
                        if peak is None:
                            total, sums = add, more
                        else:
                            shrink = jnp.exp(peak - new_peak)
                            total, sums = total * shrink + add, sums * shrink + more
                        peak = new_peak
                    lse[pair, block] = peak + jnp.log(total)
                    value = (sums * (1.0 / total)).T
                    for i in range(group_size):
                        du[q_rows, head_at(o_at, pair * group_size + i)] = value[
                            i * q_block : (i + 1) * q_block
                        ].astype(LOW)

            def project(cols):
                part[rows, cols] = dot_nn(du[rows, o_at], w_out[:, cols]).astype(LOW)

            tiled(width, 512, project)
            store.wait()
            swap1.scatter_start(c)

        def settle(c):
            value = low[swap1.rows(0, c), :].astype(F32) + swap1.scatter_result(c)
            resid[swap1.local(c), :] = value
            front_store(4 + c, resid.at[swap1.local(c)], resid_hbm.at[swap1.local(c)]).start()
            hidden[swap1.rows(0, c), :] = (unit_rows(value) * post_gain_ref[...]).astype(LOW)
            swap1.gather_start(c)

        def feed_in(c):
            rows = chunk_rows(c)

            def mask_step(local):
                at = pl.ds(c * chunk + local.start, local.size)
                grad[at, :] = jnp.where(valid(at), grad[at, :], jnp.zeros((), LOW))

            tiled(chunk, 32, mask_step)

            def unit_step(cols):
                gate = dot_nn(hidden[rows, :], wg[:, cols])
                up = dot_nn(hidden[rows, :], wu[:, cols])
                d_act = dot_nt(grad[rows, :], wd[cols, :])
                sig = jax.nn.sigmoid(gate)
                silu = gate * sig
                act[rows, cols] = (silu * up).astype(LOW)
                dg[rows, cols] = (d_act * up * sig * (1.0 + gate * (1.0 - sig))).astype(LOW)
                du[rows, cols] = (d_act * silu).astype(LOW)

            tiled(units, unit_tile, unit_step)

        def feed_back(c):
            rows = chunk_rows(c)
            swap1.scatter_end(c)

            def back_step(cols):
                part[rows, cols] = (
                    dot_nt(dg[rows, :], wg[cols, :]) + dot_nt(du[rows, :], wu[cols, :])
                ).astype(LOW)

            tiled(width, 512, back_step)

        for c in range(chunks + 1):
            if c < chunks:
                attend(c)
            if c >= 1 and c - 1 < chunks - 1:
                swap1.scatter_forward(c - 1)
                settle(c - 1)
            if c >= 2 and c - 2 < chunks - 2:
                swap1.gather_pass(c - 2, False)
        heads_store = front_store(3, du, heads_hbm)
        heads_store.start()
        resid_stores = [
            front_store(4 + c, resid.at[swap1.local(c)], resid_hbm.at[swap1.local(c)])
            for c in range(chunks)
        ]
        for item in raw_stores + feed_loads + [heads_store]:
            item.wait()
        last = chunks - 1
        swap1.gather_pass(0, True)
        feed_in(0)
        swap1.scatter_forward(last)
        settle(last)
        swap1.gather_pass(last - 1, False)
        feed_back(0)
        swap1.gather_pass(1, True)
        feed_in(1)
        swap1.gather_pass(last, False)
        feed_back(1)
        for c in range(2, chunks):
            swap1.gather_pass(c, True)
            if c == last:
                for early in range(last):
                    swap3.scatter_start(early)
            feed_in(c)
            if c < last:
                feed_back(c)
        line.fill(0, products(grad, act, (0, units, unit_tile)))
        for c in range(last):
            swap3.scatter_forward(c)
        feed_back(last)
        swap3.scatter_start(last)
        for c in range(chunks):
            swap1.gather_end(c)
            resid_stores[c].wait()


    def middle(wd, lines):
        def settle3(c):
            d_hidden = swap3.scatter_result(c)
            rows = resid[swap3.local(c), :]
            scale = inverse_norm(rows)
            add_to(post_part, jnp.sum(d_hidden * (rows * scale), axis=0, keepdims=True), c == 0)
            value = grad[swap3.rows(0, c), :].astype(F32) + rows_back(
                d_hidden * post_gain_ref[...], rows, scale
            )
            resid[swap3.local(c), :] = value
            low[swap3.rows(0, c), :] = value.astype(LOW)
            swap3.gather_start(c)

        def mix(c):
            swap3.scatter_end(c)
            rows = chunk_rows(c)

            def mix_step(cols):
                part[rows, cols] = dot_nn(act[rows, :], wd[:, cols]).astype(LOW)

            tiled(width, 512, mix_step)

        last = chunks - 1
        for c in range(last):
            settle3(c)
        line.fill(1, products(hidden, dg, (0, units, unit_tile)))
        swap3.scatter_forward(last)
        settle3(last)
        for c in range(last):
            swap3.gather_pass(c, False)
        line.tick(0, 1, lines)
        for c in range(chunks):
            mix(c)
        swap3.gather_pass(last, False)
        line.settle(lines)

    def rest(lines, total, turned, base, q_raw, k_raw, dk, dv):
        raw_loads = [
            load(1, q_raw_hbm, q_raw),
            load(2, k_raw_hbm, k_raw),
            load(3, resid_hbm, base),
        ]
        for item in raw_loads:
            item.start()
        act_load = load(0, heads_hbm, act)
        act_load.start()
        line.fill(2, products(hidden, du, (0, units, unit_tile)))
        normed_load = load(4, normed_hbm, hidden)
        normed_load.start()
        line.tick(0, 2, lines)
        for c in range(chunks):
            swap3.gather_pass(c, True)
            swap2.scatter_start(c)
        act_load.wait()

        def d_head_step(rows):
            dg[rows, o_at] = dot_nt(low[rows, :], w_out[...]).astype(LOW)

        tiled(rows_all, chunk, d_head_step)
        x_loads = [
            pltpu.make_async_copy(
                tokens_hbm.at[swap4.rows(0, c)], w_out.at[swap4.local(c)], token_sems.at[c]
            )
            for c in range(chunks)
        ]
        for item in x_loads:
            item.start()
        for item in raw_loads:
            item.wait()

        def pair_back(pair):
            for block in range(rows_all // q_block):
                rows = pl.ds(block * q_block, q_block)
                end = (block + 1) * q_block
                q2 = stacked(act, rows, q_at, pair)
                do2 = stacked(dg, rows, o_at, pair)
                keys = act[0:end, head_at(k_at, pair)]
                values = act[0:end, head_at(v_at, pair)]
                scores = dot_nt(keys, q2) * score_scale
                probs = jnp.where(
                    allowed_of(block, 0, end), jnp.exp(scores - lse[pair, block]), 0.0
                )
                d_probs = dot_nt(values, do2)
                delta = jnp.sum(probs * d_probs, axis=0, keepdims=True)
                d_scores = (probs * (d_probs - delta)).astype(LOW)
                d_value = dot_nn(probs.astype(LOW), do2)
                d_key = dot_nn(d_scores, q2)
                if block:
                    dv[0 : end - q_block, :] += d_value[: end - q_block]
                    dk[0 : end - q_block, :] += d_key[: end - q_block]
                dv[end - q_block : end, :] = d_value[end - q_block :]
                dk[end - q_block : end, :] = d_key[end - q_block :]
                d_query = (dot_tn(keys, d_scores) * score_scale).T
                for i in range(group_size):
                    head = pair * group_size + i
                    value, gain_sum = head_back(
                        d_query[i * q_block : (i + 1) * q_block],
                        q_raw[rows, pl.ds(head * head_width, head_width)],
                        cosine[rows, :],
                        sine[rows, :],
                        query_gain_ref[...],
                    )
                    dg[rows, head_at(q_at, head)] = value.astype(LOW)
                    add_to(query_part, gain_sum, head == 0 and block == 0)
            value, gain_sum = head_back(
                dk[...] * score_scale,
                k_raw[:, pl.ds(pair * head_width, head_width)],
                cosine[...],
                sine[...],
                key_gain_ref[...],
            )
            dg[:, head_at(k_at, pair)] = value.astype(LOW)
            add_to(key_part, gain_sum, pair == 0)
            dg[:, head_at(v_at, pair)] = dv[...].astype(LOW)

        store_group(0, lines, total, turned)
        for pair in range(pairs):
            pair_back(pair)
            if pair == 0:
                for c in range(chunks):
                    swap2.scatter_forward(c)
        line.tick(1, 1, lines)
        for c in range(chunks):
            rows = chunk_rows(c)

            def normed_step(cols):
                grad[rows, cols] = (
                    dot_nt(dg[rows, q_at], w_query[cols, :])
                    + dot_nt(dg[rows, k_at], w_key[cols, :])
                    + dot_nt(dg[rows, v_at], w_value[cols, :])
                ).astype(LOW)

            tiled(width, 512, normed_step)
        for c in range(chunks):
            rows = swap2.rows(0, c)
            mixed = swap2.scatter_result(c)
            part[rows, :] = jnp.where(valid(rows), base[swap2.local(c), :] + mixed, 0.0).astype(
                LOW
            )
        swap2.signal(free_sem)
        pl.semaphore_wait(free_sem, swap2.bits)
        for c in range(chunks):
            swap4.scatter_start(c)

        def own_stores(which, source, target, swap):
            return [
                pltpu.make_async_copy(
                    source.at[swap.rows(0, c), :],
                    target.at[swap.rows(0, c), :],
                    own_sems.at[which, c],
                )
                for c in range(chunks)
            ]

        own2 = own_stores(0, part, output, swap2)
        own4 = own_stores(1, grad, in_grad, swap4)
        for item in own2:
            item.start()
        normed_load.wait()
        line.tick(1, 2, lines)

        from_normed = products(hidden, dg, (0, o_at.start, heads_width))
        from_low = products(low, act, (o_at.start, units, heads_width))

        def last_tile(i):
            yield from from_normed(i)
            yield from from_low(i)

        line.fill(3, last_tile)
        for c in range(chunks):
            swap4.scatter_forward(c)
        store_group(1, lines, total, turned)
        for item in x_loads:
            item.wait()
        for c in range(chunks):
            local = swap4.local(c)
            d_normed = swap4.scatter_result(c)
            x = w_out[local, :].astype(F32)
            scale = inverse_norm(x)
            add_to(in_part, jnp.sum(d_normed * (x * scale), axis=0, keepdims=True), c == 0)
            value = resid[local, :] + rows_back(d_normed * in_gain_ref[...], x, scale)
            grad[swap4.rows(0, c), :] = value.astype(LOW)
            swap4.gather_start(c)
            own4[c].start()
        steps = len(spread.steps)
        spread.copy(0).start()
        for c in range(chunks):
            swap4.gather_pass(c, False)
        line.tick(2, 1, lines)
        for c in range(chunks):
            swap2.gather_start(c)
        spread.next(0)
        spread.next(1)
        for c in range(chunks):
            swap2.gather_pass(c, False)
        line.tick(2, 2, lines)
        for step in range(2, steps):
            spread.next(step)
        gains_out[...] = spread.mine[steps]
        for c in range(chunks):
            swap4.gather_pass(c, True)
        store_group(2, lines, total, turned)
        for c in range(chunks):
            swap2.gather_pass(c, True)
        for step in range(1, line.places - 1):
            line.tick(3, step, lines)
        store_group(3, lines, total, turned)
        for item in own2 + own4:
            item.wait()
        for c in range(chunks):
            swap3.gather_end(c)
            for swap in (swap2, swap4):
                swap.scatter_end(c)
                swap.gather_end(c)
        for group in range(line.groups):
            line.ends(group, "wait")

    def store_group(group, lines, total, turned):
        line.finish(group, lines, total)
        if group == 0:
            turned[...] = total[...].T
            copies = [(turned, down_out)]
        elif group == 3:
            turned[0:heads_width, :] = total[:, o_at].T
            copies = [
                (total.at[:, q_at], query_out),
                (total.at[:, k_at], key_out),
                (total.at[:, v_at], value_out),
                (turned.at[pl.ds(0, heads_width), :], proj_out),
            ]
        else:
            copies = [(total, (gate_out, up_out)[group - 1])]
        copies = [
            pltpu.make_async_copy(src, dst, final_sems.at[i])
            for i, (src, dst) in enumerate(copies)
        ]
        for copy in copies:
            copy.start()
        for copy in copies:
            copy.wait()

    def both(wd):
        pl.run_scoped(
            functools.partial(front, wd),
            pltpu.VMEM((width, units), LOW),
            pltpu.VMEM((width, units), LOW),
            pltpu.VMEM((chunk, heads_width), F32),
            pltpu.VMEM((chunk, keys_width), F32),
        )
        pl.run_scoped(functools.partial(middle, wd), lines)

    lines = pltpu.VMEM((2, 2, line.tile, line.width), LOW)
    pl.run_scoped(both, pltpu.VMEM((units, width), LOW))
    pl.run_scoped(
        rest,
        lines,
        pltpu.VMEM((line.tile, line.width), F32),
        pltpu.VMEM((line.width, line.tile), F32),
        pltpu.VMEM(resid.shape, F32),
        pltpu.VMEM((rows_all, heads_width), F32),
        pltpu.VMEM((rows_all, keys_width), F32),
        pltpu.VMEM((rows_all, head_width), F32),
        pltpu.VMEM((rows_all, head_width), F32),
    )


def layer_call(counts, sizes, length, gains, tokens, out_grad, tables, attn_weights, feed_weights):
    tensor_count, dp_count = counts
    q_block, head_width, pairs, group_size = sizes
    rows, width = tokens.shape
    units = feed_weights[0].shape[1]
    heads_width, keys_width = attn_weights[0].shape[1], attn_weights[1].shape[1]
    tile = width // dp_count
    swaps = [Swap(tensor_count, rows, width) for _ in range(4)]
    line = Line(dp_count, 4, tile, units)
    spread = Spread(counts, 2 * width + 2 * head_width)
    chunks = swaps[0].chunks
    wide = jax.ShapeDtypeStruct((rows, width), LOW)
    out_shape = (
        wide,
        wide,
        jax.ShapeDtypeStruct((1, spread.length), F32),
        jax.ShapeDtypeStruct((units, tile), F32),
        jax.ShapeDtypeStruct((tile, units), F32),
        jax.ShapeDtypeStruct((tile, units), F32),
        jax.ShapeDtypeStruct((tile, heads_width), F32),
        jax.ShapeDtypeStruct((tile, keys_width), F32),
        jax.ShapeDtypeStruct((tile, keys_width), F32),
        jax.ShapeDtypeStruct((heads_width, tile), F32),
        *line.outputs(),
        wide,
        jax.ShapeDtypeStruct((rows, 2 * heads_width + 2 * keys_width), LOW),
        jax.ShapeDtypeStruct((rows, heads_width), F32),
        jax.ShapeDtypeStruct((rows, keys_width), F32),
        jax.ShapeDtypeStruct((chunks * swaps[0].block, width), F32),
    )
    big = pltpu.VMEM((rows, width), LOW)
    inner = pltpu.VMEM((rows, units), LOW)
    return pl.pallas_call(
        functools.partial(layer_kernel, (*swaps, line, spread, sizes)),
        out_shape=out_shape,
        in_specs=[pl.BlockSpec(memory_space=pltpu.SMEM)] + [vmem_spec()] * 4 + [any_spec()] * 11,
        out_specs=(any_spec(),) * 2 + (vmem_spec(),) + (any_spec(),) * 15,
        scratch_shapes=[
            big,
            big,
            inner,
            inner,
            inner,
            big,
            big,
            pltpu.VMEM((chunks * swaps[0].block, width), F32),
            pltpu.VMEM((2, tile, units), LOW),
            pltpu.VMEM((tile, units), LOW),
            pltpu.VMEM((tile, rows), LOW),
            swaps[0].landing(),
            pltpu.VMEM((width, heads_width), LOW),
            pltpu.VMEM((width, keys_width), LOW),
            pltpu.VMEM((width, keys_width), LOW),
            pltpu.VMEM((heads_width, width), LOW),
            pltpu.VMEM((rows, head_width), F32),
            pltpu.VMEM((rows, head_width), F32),
            pltpu.VMEM((pairs, rows // q_block, 1, group_size * q_block), F32),
            pltpu.SemaphoreType.DMA((10,)),
            pltpu.SemaphoreType.DMA((chunks,)),
            pltpu.SemaphoreType.DMA((4 + chunks,)),
            pltpu.SemaphoreType.DMA((2, chunks)),
            pltpu.SemaphoreType.DMA((4,)),
            pltpu.SemaphoreType.REGULAR,
            *[item for swap in swaps for item in swap.semaphores()],
            *line.semaphores(),
            *spread.scratch(),
        ],
        compiler_params=kernel_params(0),
        name="layer",
    )(length, *gains, tokens, out_grad, *tables, *attn_weights, *feed_weights)[:10]


def rope_tables(head_width, row_count):
    half_width = head_width // 2
    inv_freq = ROPE_BASE ** (-2.0 * np.arange(half_width, dtype=np.float32) / head_width)
    angles = np.arange(row_count, dtype=np.float32)[:, None] * inv_freq.astype(np.float32)[None, :]
    cosine, sine = np.cos(angles), np.sin(angles)
    tables = np.concatenate([cosine, cosine], 1), np.concatenate([-sine, sine], 1)
    return tuple(jnp.asarray(table, F32) for table in tables)


def on_device(
    tensor_count,
    dp_count,
    tokens,
    lengths,
    in_gain,
    w_query,
    w_key,
    w_value,
    query_gain,
    key_gain,
    w_out,
    post_gain,
    w_gate,
    w_up,
    w_down,
    out_grad,
):
    head_width = query_gain.shape[0]
    pairs = w_key.shape[1] // head_width
    group_size = w_query.shape[1] // w_key.shape[1]
    q_block = min(128, tokens.shape[0])
    (
        output,
        in_grad,
        gains,
        grad_down,
        grad_gate,
        grad_up,
        grad_query,
        grad_key,
        grad_value,
        grad_out,
    ) = layer_call(
        (tensor_count, dp_count),
        (q_block, head_width, pairs, group_size),
        lengths,
        (in_gain[None], post_gain[None], query_gain[None], key_gain[None]),
        tokens,
        out_grad,
        rope_tables(head_width, tokens.shape[0]),
        (w_query, w_key, w_value, w_out),
        (w_gate, w_up, w_down),
    )
    width = tokens.shape[1]
    cuts = (width, 2 * width, 2 * width + head_width)
    grad_post_gain, grad_in_gain, grad_query_gain, grad_key_gain = jnp.split(gains[0], cuts)
    return (
        output,
        in_grad,
        grad_in_gain,
        grad_query,
        grad_key,
        grad_value,
        grad_query_gain,
        grad_key_gain,
        grad_out,
        grad_post_gain,
        grad_gate,
        grad_up,
        grad_down,
    )


def solution(mesh):
    tensor_count, dp_count = mesh.shape["tensor"], mesh.shape["dp"]

    def layer(*args):
        return on_device(tensor_count, dp_count, *args)

    return jax.shard_map(
        layer,
        mesh=mesh,
        in_specs=(
            P("dp", None),
            P("dp"),
            P(),
            P(None, "tensor"),
            P(None, "tensor"),
            P(None, "tensor"),
            P(),
            P(),
            P("tensor", None),
            P(),
            P(None, "tensor"),
            P(None, "tensor"),
            P("tensor", None),
            P("dp", None),
        ),
        out_specs=(
            P("dp", None),
            P("dp", None),
            P(),
            P("dp", "tensor"),
            P("dp", "tensor"),
            P("dp", "tensor"),
            P(),
            P(),
            P("tensor", "dp"),
            P(),
            P("dp", "tensor"),
            P("dp", "tensor"),
            P("tensor", "dp"),
        ),
        check_vma=False,
    )
```

time: 549 us -> 426 us (0.78)
  the two profiles are of different devices: /device:TPU:0 before, /device:TPU:20 now
where the time goes in v3:
time: 426 us; the launch traced here: 418 us
  Pallas kernels  400 us (94%)
  local copies, waits for them, and re-layouts  16 us (4%)
    pallas_call x1, Pallas kernels, layer_call(): pl.pallas_call(functools.partial(layer_kernel, (*swaps, line, spread, siz...  400 us
    unnamed x25, local copies, waits for them, and re-layouts  13.5 us

profile of v3, /device:TPU:20, one launch (start us, length us, event | category | flops | bytes accessed | tf_op | source)
XLA Modules:
  0.0 417.7 jit_solution(174618528469896215)
XLA Ops:
  1.3 399.9 %layer.1 = (bf16[1024,2048]{1,0:T(8,128)(2,1)}, bf16[1024,2048]{1,0:T(8,128)(2,1)}, f32[1,4352]{1,0:T(1,128)}, f32[1536,256]{1,0:T(8,128)}, f32[256,1536]{1,0:T(...) custom-call(s32[1]{0:T(128)S(6)} %copy.38.refs_0_, ...), custom_call_target="tpu_custom_call" | custom-call | tf_op jit(solution)/shard_map/layer/pallas_call | solution.py:1079
  401.2 1.2 slice_bitcast_fusion
  402.4 1.3 fusion
  403.7 0.0 copy-start
  403.7 4.9 %copy.39 = bf16[1024,2048]{1,0:T(8,128)(2,1)} copy(bf16[1024,2048]{1,0:T(8,128)(2,1)} %get-tuple-element.50) | data formatting | bytes 8388608
  408.6 0.0 copy-done
  408.6 0.0 copy-start.5
  408.6 0.0 copy-start.7
  408.6 0.0 copy-start.6
  408.6 0.0 copy-start.4
  408.6 0.0 copy-start.3
  408.7 2.1 copy.40
  410.8 0.0 copy-done.5
  410.8 0.0 copy-start.2
  410.8 0.8 copy.41
  411.6 0.0 copy-done.7
  411.6 0.0 copy-start.1
  411.6 0.7 copy.42
  412.3 0.0 copy-done.6
  412.3 0.7 copy.43
  413.0 0.0 copy-done.4
  413.0 0.8 copy.44
  413.8 0.0 copy-done.3
  413.8 1.1 copy.45
  414.9 0.0 copy-done.2
  415.0 1.1 copy.46
  416.1 0.0 copy-done.1
  416.1 1.1 copy.47
Async XLA Ops:
  403.7 4.9 %copy-start = (bf16[1024,2048]{1,0:T(8,128)(2,1)S(1)}, bf16[1024,2048]{1,0:T(8,128)(2,1)}, u32[]{:S(2)}) copy-start(bf16[1024,2048]{1,0:T(8,128)(2,1)} %get-tuple-element.51) | copy-start | bytes 12582916
  408.6 2.2 copy-start.5
  408.6 3.0 copy-start.7
  408.6 3.7 copy-start.6
  408.6 4.4 %copy-start.4 = (f32[512,256]{1,0:T(8,128)S(1)}, f32[512,256]{1,0:T(8,128)}, u32[]{:S(2)}) copy-start(f32[512,256]{1,0:T(8,128)} %get-tuple-element.58) | copy-start | bytes 1572868
  408.6 5.2 %copy-start.3 = (f32[256,1536]{1,0:T(8,128)S(1)}, f32[256,1536]{1,0:T(8,128)}, u32[]{:S(2)}) copy-start(f32[256,1536]{1,0:T(8,128)} %get-tuple-element.60) | copy-start | bytes 4718596
  410.8 4.2 copy-start.2
  411.6 4.5 %copy-start.1 = (f32[1536,256]{1,0:T(8,128)S(1)}, f32[1536,256]{1,0:T(8,128)}, u32[]{:S(2)}) copy-start(f32[1536,256]{1,0:T(8,128)} %get-tuple-element.62) | copy-start | bytes 4718596
